TPU v7x, 512 devices: a whole 4x8x8 slice. The times are simulated.
512 devices in a mesh: dev: 128 (over z, y, core), rep: 4 (over x).
Axes of the slice: x: 4, y: 8, z: 8, core: 2. Of those that a mesh axis runs over, the one named last changes fastest.
Arguments:
- params: float32 [10, 65536], P(None, 'dev'), may hold values from -8 to 6
- moment1: float32 [10, 65536], P(None, 'dev'), may hold values from -0.06 to 0.06
- moment2: float32 [10, 65536], P(None, 'dev'), may hold values from 0.0001 to 0.01
- camera: float32 [4, 8], P('rep'), may hold values from -3 to 3
- owner: int32 [4, 256, 512, 1], P('rep', 'dev'), may hold values from 0 to 127; in each aligned block of 1024 rows (0 to 1023, 1024 to 2047, ..., all dimensions but the last counted through in order) at most 16 rows name the same one
- local_index: int32 [4, 256, 512], P('rep', 'dev'), may hold values from 0 to 511
- target: float32 [4, 256, 3, 256], P('rep', 'dev'), may hold values from 0 to 1
- rehome: int32 [128, 128], P('dev'), may hold values from 0 to 127, each once within a row
Outputs:
- params_next: float32 [10, 65536], P(None, 'dev')
- moment1_next: float32 [10, 65536], P(None, 'dev')
- moment2_next: float32 [10, 65536], P(None, 'dev')
- rendered: float32 [4, 256, 3, 256], P('rep', 'dev')
Inputs may be any that keep to these rules, and one draw needn't show every extreme that they name: In the entries of one device's tiles of one camera (aligned blocks of 1024 entries) no owner is named more than 16 times, a bound that some block reaches. `rehome`: each row is a permutation of the devices.
All inputs are finite; a program needn't handle non-finite values.
Results may differ from a plain program's by a relative error of at most 0.00014.
Values sent between devices are 32-bit elements; how exact they have to be, the bound alone decides.
No kernel may reach another device: no remote copies, remote signals or barrier semaphores. Data moves between devices by JAX's collectives and lax.ppermute only.
A program may use at most 128 MiB of HBM per device.

v0:
```python
import functools

import jax
import jax.numpy as jnp
from jax import lax
from jax.sharding import PartitionSpec as P

SIDE = 16
PIX = 256


BACKGROUND = 0.5


def project(params, camera_row):
    xpos = params[0]
    ypos = params[1]
    zpos = params[2]
    screen_u = camera_row[0] * xpos + camera_row[1] * ypos + camera_row[2] * zpos + camera_row[3]
    screen_v = camera_row[4] * xpos + camera_row[5] * ypos + camera_row[6] * zpos + camera_row[7]
    conic_a = jnp.exp(params[3])
    conic_c = jnp.exp(params[5])
    conic_b = 0.9 * jnp.tanh(params[4]) * jnp.sqrt(conic_a * conic_c)
    opacity = jax.nn.sigmoid(params[6])
    colors = jax.nn.sigmoid(params[7:10])
    head = jnp.stack([screen_u, screen_v, conic_a, conic_b, conic_c, opacity])
    return jnp.concatenate([head, colors], axis=0)


def render(values):
    pixel_ids = jnp.arange(PIX)
    column = (pixel_ids % SIDE).astype(jnp.float32) - 7.5
    row_pos = (pixel_ids // SIDE).astype(jnp.float32) - 7.5
    delta_u = column[None, :, None] - values[:, 0][:, None, :]
    delta_v = row_pos[None, :, None] - values[:, 1][:, None, :]
    quad = (
        values[:, 2][:, None, :] * delta_u * delta_u
        + 2.0 * values[:, 3][:, None, :] * delta_u * delta_v
        + values[:, 4][:, None, :] * delta_v * delta_v
    )
    alpha = 0.99 * values[:, 5][:, None, :] * jnp.exp(-0.5 * quad)
    log_keep = jnp.log(1.0 - alpha)
    running = jnp.cumsum(log_keep, axis=2)
    weight = alpha * jnp.exp(running - log_keep)
    image = jnp.einsum("bpk,bck->bcp", weight, values[:, 6:9], precision=lax.Precision.HIGHEST)
    return image + BACKGROUND * jnp.exp(running[:, :, -1])[:, None, :]


def local(params, moment1, moment2, camera, owner, local_index, target, rehome):
    devices = lax.axis_size("dev")
    gauss_dev = params.shape[1]
    tiles_dev = local_index.shape[1]
    list_len = local_index.shape[2]
    projected, pullback = jax.vjp(functools.partial(project, camera_row=camera[0]), params)
    destination = owner[0, :, :, 0].reshape(-1)
    local_ids = local_index[0].reshape(-1)
    whole = lax.all_gather(projected, "dev", axis=1, tiled=True)
    global_ids = destination * gauss_dev + local_ids
    entries = jnp.take(whole, global_ids, axis=1)
    values = (
        entries.reshape(9, tiles_dev, list_len)
        .transpose(1, 0, 2)
        .reshape(tiles_dev // 2, 2, 9, list_len)
    )
    goals = target[0].reshape(tiles_dev // 2, 2, 3, PIX)

    def one_block(pair):
        block_values, block_target = pair
        image, pull_render = jax.vjp(render, block_values)
        return (image, pull_render(image - block_target)[0])

    images, grad_values = lax.map(one_block, (values, goals))
    grad_entries = grad_values.reshape(tiles_dev, 9, list_len).transpose(1, 0, 2).reshape(9, -1)
    spread = jnp.zeros((9, gauss_dev * devices), jnp.float32).at[:, global_ids].add(grad_entries)
    grad_table = lax.psum_scatter(spread, "dev", scatter_dimension=1, tiled=True)
    grad_local = pullback(grad_table)[0]
    grad_total = lax.psum(grad_local, "rep")
    moment1_new = 0.9 * moment1 + 0.1 * grad_total
    moment2_new = 0.99 * moment2 + 0.01 * grad_total * grad_total
    params_new = params - 0.01 * moment1_new / (jnp.sqrt(moment2_new) + 1e-08)
    stacked = jnp.stack([params_new, moment1_new, moment2_new]).reshape(
        3, 10, devices, gauss_dev // devices
    )
    block_ids = jnp.arange(devices, dtype=jnp.int32)
    matches = (rehome[0][:, None] == block_ids[None, :]).astype(jnp.int32)
    inverse = jnp.sum(matches * block_ids[:, None], axis=0)
    outgoing_blocks = jnp.take(stacked, inverse, axis=2)
    arrived = lax.all_to_all(
        outgoing_blocks, "dev", split_axis=2, concat_axis=2, tiled=True
    ).reshape(3, 10, gauss_dev)
    return (arrived[0], arrived[1], arrived[2], images)


def solution(mesh):
    in_specs = (
        P(None, "dev"),
        P(None, "dev"),
        P(None, "dev"),
        P("rep", None),
        P("rep", "dev", None, None),
        P("rep", "dev", None),
        P("rep", "dev", None, None),
        P("dev", None),
    )
    out_specs = (P(None, "dev"), P(None, "dev"), P(None, "dev"), P("rep", "dev", None, None))
    return jax.shard_map(local, mesh=mesh, in_specs=in_specs, out_specs=out_specs, check_vma=False)
```

profile of v0, /device:TPU:1, one launch (start us, length us, event | category | flops | bytes accessed | tf_op | source)
XLA Modules:
  0.0 469.1 jit_solution(8419153605545001573)
XLA Ops:
  7.2 1.6 fusion.66
  8.9 0.8 add_divide_fusion
  9.6 3.5 add_divide_fusion.1
  13.1 3.5 add_add_fusion
  16.6 2.0 concatenate.4
  18.7 0.7 fusion.47
  19.4 0.7 copy.274
  20.1 0.7 compare_and_fusion
  20.8 88.6 %all-gather.2.cloned.1.call-done = f32[9,65536]{1,0:T(8,128)} async-done(((f32[9,512]{1,0:T(8,128)}), f32[9,65536]{1,0:T(8,128)}) %all-gather.2.cloned.1.call-update) | async-done | bytes 2359312 | tf_op jit(solution)/shard_map/all_gather | solution.py:57
  109.4 16.9 %copy.241 = f32[9,65536]{0,1:T(8,128)} copy(f32[9,65536]{1,0:T(8,128)} %all-gather.2.cloned.1.call-done) | data formatting | bytes 4718592 | tf_op jit(solution)/shard_map/all_gather | solution.py:57
  126.4 13.3 %gather_fusion = f32[1024,9]{1,0:T(8,128)S(1)} fusion(f32[9,65536]{0,1:T(8,128)} %copy.241, s32[1024]{0:T(1024)S(1)} %broadcast_clamp_fusion), kind=kCustom, calls=%fused_computation | custom fusion | bytes 77824 | tf_op jit(solution)/shard_map/jit(_take)/gather | solution.py:59
  139.7 0.2 copy.243
  140.9 1.8 fusion.18
  142.7 0.2 broadcast_add_fusion.1
  142.9 0.6 copy.250
  143.5 0.4 reduce_window_sum.33
  143.9 0.3 multiply_reduce_fusion.1
  144.2 1.7 fusion.63
  146.0 1.4 fusion.39
  147.4 0.2 copy.252
  147.5 0.2 fusion.38
  147.7 2.8 pad_add_fusion
  150.5 0.4 reshape.269
  150.8 0.8 copy.253
  151.6 4.3 fusion.67
  156.0 0.2 broadcast_add_fusion
  156.2 0.6 copy.254
  156.8 0.4 reduce_window_sum.35
  157.2 3.2 fusion.24
  160.7 0.2 copy.256
  160.9 19.2 %scatter_custom_fusion = f32[9,65536]{0,1:T(8,128)} fusion(s32[1024]{0:T(1024)S(1)} %bitcast.99, f32[1024,9]{1,0:T(8,128)S(1)} %copy.256, f32[]{:T(128)} %constant.106.clone.1), kind=kCustom, calls=%fused_computation.3 | custom fusion | flops 9216 | bytes 2359300 | tf_op jit(solution)/shard_map/scatter-add | solution.py:74
  180.1 19.4 %copy.257 = f32[9,65536]{1,0:T(8,128)} copy(f32[9,65536]{0,1:T(8,128)} %scatter_custom_fusion) | data formatting | bytes 4718592 | tf_op jit(solution)/shard_map/scatter-add | solution.py:74
  199.7 193.2 %reduce-scatter.2.cloned.1.call-done = f32[9,512]{1,0:T(8,128)} async-done(((f32[9,65536]{1,0:T(8,128)}), f32[9,512]{1,0:T(8,128)}) %reduce-scatter.2.cloned.1.call-update) | async-done | bytes 18448 | tf_op jit(solution)/shard_map/reduce_scatter | solution.py:75
  392.9 4.7 fusion.48
  397.6 0.8 fusion.46
  398.3 0.8 multiply_multiply_fusion.4
  399.2 13.2 %psum.7 = f32[10,512]{1,0:T(8,128)S(1)} all-reduce(f32[10,512]{1,0:T(8,128)S(1)} %pad_add_fusion.1), channel_id=1, replica_groups=mesh['dev'=128,'rep'=4] {'rep'}, use_global_device_ids=true, to_apply=%region_14.15 | all-reduce | flops 5120 | bytes 40960 | tf_op jit(solution)/shard_map/psum | solution.py:77
  412.6 0.1 copy.259
  412.8 0.1 copy.260
  412.9 0.2 pad_maximum_fusion
  413.2 1.1 gather_fusion.1
  414.3 1.1 select_bitcast_fusion
  415.4 18.6 %all-to-all-start = ((f32[3,10,128,4]{1,3,0,2:T(4,128)}), f32[3,10,128,4]{1,3,0,2:T(4,128)S(1)}, u32[]{:S(2)}, u32[]{:S(2)}) async-start(f32[3,10,128,4]{1,3,0,2:T(4,128)} %select_bitcast_fusion), calls=%async_computation.1 | async-start | bytes 1572864 | tf_op jit(solution)/shard_map/all_to_all | solution.py:88
  434.0 0.6 copy.264
  434.6 25.3 %all-to-all-done = f32[3,10,128,4]{1,3,0,2:T(4,128)S(1)} async-done(((f32[3,10,128,4]{1,3,0,2:T(4,128)}), f32[3,10,128,4]{1,3,0,2:T(4,128)S(1)}, u32[]{:S(2)}, u32[]{:S(2)}) %all-to-all-start) | async-done | bytes 61472 | tf_op jit(solution)/shard_map/all_to_all | solution.py:88
  460.1 0.7 copy.261
  460.8 0.7 copy.262
  461.6 0.7 copy.263
  (58 shorter events, 1.8 us)
Async XLA Ops:
  7.2 137.1 %copy-start.3 = (f32[1,2,3,256]{3,1,2,0:T(2,128)S(1)}, f32[1,2,3,256]{3,1,2,0:T(2,128)}, u32[]{:S(2)}) copy-start(f32[1,2,3,256]{3,1,2,0:T(2,128)} %param.14) | copy-start | bytes 18436
  7.2 102.3 %all-gather.2.cloned.1.call-start = ((), (), s32[]{:S(2)}) async-start(), calls=%async_computation.2 | async-start | bytes 4227072 | tf_op jit(solution)/shard_map/all_gather | solution.py:57
  18.6 374.2 %reduce-scatter.2.cloned.1.call-start = ((), (), s32[]{:S(2)}) async-start(), calls=%async_computation.3 | async-start | bytes 4227072 | tf_op jit(solution)/shard_map/reduce_scatter | solution.py:75
  160.9 38.7 %copy-start.4 = (s32[1,128]{1,0:T(1,128)S(1)}, s32[1,128]{1,0:T(1,128)}, u32[]{:S(2)}) copy-start(s32[1,128]{1,0:T(1,128)} %param.15) | copy-start | bytes 1540
  160.9 232.0 %copy-start = (f32[10,512]{1,0:T(8,128)S(1)}, f32[10,512]{1,0:T(8,128)}, u32[]{:S(2)}) copy-start(f32[10,512]{1,0:T(8,128)} %param.8) | copy-start | bytes 61444
  160.9 251.5 %copy-start.1 = (f32[10,512]{1,0:T(8,128)S(1)}, f32[10,512]{1,0:T(8,128)}, u32[]{:S(2)}) copy-start(f32[10,512]{1,0:T(8,128)} %param.9) | copy-start | bytes 61444
  160.9 251.5 %copy-start.2 = (f32[10,512]{1,0:T(8,128)S(1)}, f32[10,512]{1,0:T(8,128)}, u32[]{:S(2)}) copy-start(f32[10,512]{1,0:T(8,128)} %param.10) | copy-start | bytes 61444
  415.4 44.5 %all-to-all-start = ((f32[3,10,128,4]{1,3,0,2:T(4,128)}), f32[3,10,128,4]{1,3,0,2:T(4,128)S(1)}, u32[]{:S(2)}, u32[]{:S(2)}) async-start(f32[3,10,128,4]{1,3,0,2:T(4,128)} %select_bitcast_fusion), calls=%async_computation.1 | async-start | bytes 1572864 | tf_op jit(solution)/shard_map/all_to_all | solution.py:88
Sparse Core Ops, SparseCore 0:
  18.8 90.6 all-gather.1
  199.7 193.1 reduce-scatter.1
where the time goes:
time: 471 us; the launch traced here: 469 us
  waiting for transfers between devices  307 us (65%)
  local copies, waits for them, and re-layouts  63.2 us (13%)
  other arithmetic  46.4 us (10%)
  starting transfers between devices  18.7 us (4%)
  between operations  14.6 us (3%)
  blocking collectives  13.2 us (3%)
  matrix products  5.91 us (1%)
    reduce_scatter x1, waiting for transfers between devices, local(): lax.psum_scatter(spread, 'dev', scatter_dimension=1, tiled=True)  193 us
    all_gather x1, waiting for transfers between devices, local(): whole = lax.all_gather(projected, 'dev', axis=1, tiled=True)  88.6 us
    all_to_all x1, waiting for transfers between devices, local(): lax.all_to_all(outgoing_blocks, 'dev', split_axis=2, concat_axis=2, tiled...  25.3 us
    scatter-add x1, local copies, waits for them, and re-layouts, local(): jnp.zeros((9, gauss_dev * devices), jnp.float32).at[:, global_ids]  19.4 us
    scatter-add x1, other arithmetic, local(): jnp.zeros((9, gauss_dev * devices), jnp.float32).at[:, global_ids]  19.2 us
    all_to_all x1, starting transfers between devices, local(): lax.all_to_all(outgoing_blocks, 'dev', split_axis=2, concat_axis=2, tiled...  18.6 us
    all_gather x1, local copies, waits for them, and re-layouts, local(): whole = lax.all_gather(projected, 'dev', axis=1, tiled=True)  16.9 us
    gather x2, local copies, waits for them, and re-layouts, local(): entries = jnp.take(whole, global_ids, axis=1)  13.5 us
  transfers between devices with their start and end apart: 3, of which 3 were waited for; matrix products, arithmetic and copies ran while one was open for 1% of the time, Pallas kernels for 0%

commit v1 on v0

v1 whole, which is shorter than its diff:
```python
import functools

import jax
import jax.numpy as jnp
from jax import lax
from jax.experimental import pallas as pl
from jax.experimental.pallas import tpu as pltpu
from jax.sharding import PartitionSpec as P

SIDE = 16
BACKGROUND = 0.5
CAP = 16
ROWS = 16
VMEM = 48 * 1024 * 1024
F32 = jnp.float32
BF16 = jnp.bfloat16


def one_hot(condition):
    return jnp.where(condition, 1.0, 0.0).astype(BF16)


def parts(x, count=3):
    out = []
    for _ in range(count):
        piece = x.astype(BF16)
        out.append(piece)
        x = x - piece.astype(F32)
    return out


def iota(shape, dim):
    return lax.broadcasted_iota(jnp.int32, shape, dim)


def dot(a, b):
    return lax.dot_general(a, b, (((1,), (0,)), ((), ())), preferred_element_type=F32)


def dot_t(a, b):
    return lax.dot_general(a, b, (((1,), (1,)), ((), ())), preferred_element_type=F32)


def call(body, out_shape, scratch=(), smem=()):
    def run(*args):
        specs = [
            pl.BlockSpec(memory_space=pltpu.SMEM if i in smem else pltpu.VMEM)
            for i in range(len(args))
        ]
        outs = jax.tree.map(lambda _: pl.BlockSpec(memory_space=pltpu.VMEM), out_shape)
        return pl.pallas_call(
            body,
            out_shape=out_shape,
            in_specs=specs,
            out_specs=outs,
            scratch_shapes=list(scratch),
            compiler_params=pltpu.CompilerParams(vmem_limit_bytes=VMEM),
        )(*args)

    return run


def request_body(owner_ref, index_ref, request_ref, rank_ref):
    entries = owner_ref.shape[1]
    devices = request_ref.shape[0]
    step = 256
    before = one_hot(iota((step, step), 0) < iota((step, step), 1))
    base = jnp.zeros((devices, 1), F32)
    total = jnp.zeros((devices, 2 * CAP), F32)
    for start in range(0, entries, step):
        owner = owner_ref[:, start : start + step]
        ids = index_ref[:, start : start + step]
        named = jnp.where(iota((devices, step), 0) == owner, 1.0, 0.0)
        named_b = named.astype(BF16)
        count = dot(named_b, before) + base
        base = base + jnp.sum(named, axis=1, keepdims=True)
        rank = jnp.sum(named * count, axis=0, keepdims=True).astype(jnp.int32)
        rank_ref[:, start : start + step] = rank
        slot = iota((CAP, step), 0) == rank
        high = jnp.where(slot, (ids >> 4).astype(F32), 0.0)
        low = jnp.where(slot, (ids & 15).astype(F32), 0.0)
        total = total + dot_t(named_b, jnp.concatenate([high, low], axis=0).astype(BF16))
    ids = 16.0 * total[:, :CAP] + total[:, CAP:]
    request_ref[...] = jnp.concatenate(
        [ids, jnp.zeros((devices, request_ref.shape[1] - CAP), F32)], axis=1
    )


def asked_hot(request_ref, gauss):
    devices = request_ref.shape[0]
    ids = jnp.transpose(request_ref[...]).astype(jnp.int32)
    return jnp.concatenate(
        [one_hot(iota((gauss, devices), 0) == ids[j : j + 1]) for j in range(CAP)], axis=1
    )


def conics(params_ref):
    conic_a = jnp.exp(params_ref[3:4])
    conic_c = jnp.exp(params_ref[5:6])
    skew = jnp.tanh(params_ref[4:5])
    return conic_a, conic_c, skew, jnp.sqrt(conic_a * conic_c)


def sigmoid(x):
    return 1.0 / (1.0 + jnp.exp(-x))


def respond_body(request_ref, params_ref, camera_ref, response_ref, table):
    gauss = params_ref.shape[1]
    devices = request_ref.shape[0]
    cam = [camera_ref[0, i] for i in range(8)]
    x, y, z = params_ref[0:1], params_ref[1:2], params_ref[2:3]
    conic_a, conic_c, skew, root = conics(params_ref)
    table[...] = jnp.zeros_like(table)
    table[0:1] = cam[0] * x + cam[1] * y + cam[2] * z + cam[3]
    table[1:2] = cam[4] * x + cam[5] * y + cam[6] * z + cam[7]
    table[2:3] = conic_a
    table[3:4] = 0.9 * skew * root
    table[4:5] = conic_c
    table[5:9] = sigmoid(params_ref[6:10])
    hot = asked_hot(request_ref, gauss)
    got = dot(jnp.concatenate(parts(table[...]), axis=0), hot)
    got = got[:ROWS] + got[ROWS : 2 * ROWS] + got[2 * ROWS :]
    for half in range(2):
        block = jnp.concatenate(
            [got[:, j * devices : (j + 1) * devices] for j in range(half * 8, half * 8 + 8)],
            axis=0,
        )
        response_ref[:, half * 128 : half * 128 + 128] = jnp.transpose(block)


def composite_body(
    response_ref, owner_ref, rank_ref, target_ref, image_ref, grad_ref,
    alpha_s, run_s, weight_s, split_s, goal_s, image_s, tail_s, entry_s,
):
    devices = response_ref.shape[0]
    entries = owner_ref.shape[1]
    tiles, _, pix = target_ref.shape
    depth = entries // tiles
    owner, rank = owner_ref[...], rank_ref[...]
    named = one_hot(iota((devices, entries), 0) == owner)
    got = jnp.concatenate(
        [jnp.transpose(response_ref[:, :128]), jnp.transpose(response_ref[:, 128:])], axis=0
    )
    spread = sum(dot(piece, named) for piece in parts(got))
    values = jnp.zeros((ROWS, entries), F32)
    for j in range(CAP):
        values = values + jnp.where(rank == j, spread[j * ROWS : (j + 1) * ROWS], 0.0)
    pad = jnp.zeros((5, pix), F32)
    for t in range(tiles):
        goal_s[t * pix : (t + 1) * pix, 0:8] = jnp.transpose(
            jnp.concatenate([target_ref[t], pad], axis=0)
        )
    rows_of = []
    for t in range(tiles):
        rows_of.append([values[r : r + 1, t * depth : (t + 1) * depth] for r in range(9)])
    across = iota((SIDE, depth), 0).astype(F32) - 7.5

    def chunk(t, i):
        return pl.ds(pl.multiple_of(t * pix + i * SIDE, SIDE), SIDE)

    deltas = []
    for t in range(tiles):
        u, v, conic_a, conic_b, conic_c, opacity = rows_of[t][:6]
        delta_u = across - u
        deltas.append(delta_u)
        first = (-0.5 * conic_a) * delta_u * delta_u
        mixed = -conic_b * delta_u
        half_c = -0.5 * conic_c
        peak = 0.99 * opacity

        def forward(i, carry, t=t, v=v, first=first, mixed=mixed, half_c=half_c, peak=peak):
            delta_v = (i.astype(F32) - 7.5) - v
            power = first + delta_v * (mixed + half_c * delta_v)
            alpha = peak * jnp.exp(power)
            log_keep = jnp.log(1.0 - alpha)
            alpha_s[chunk(t, i)] = alpha
            for n, piece in enumerate(parts(log_keep)):
                split_s[n, chunk(t, i)] = piece
            return carry

        lax.fori_loop(0, pix // SIDE, forward, 0)
    earlier = one_hot(iota((depth, depth), 0) < iota((depth, depth), 1))
    run_s[...] = sum(dot(split_s[n], earlier) for n in range(3))
    color_grads = []
    for t in range(tiles):
        colors = rows_of[t][6:9]

        def shade(i, sums, t=t, colors=colors):
            rows = chunk(t, i)
            alpha = alpha_s[rows]
            through = jnp.exp(run_s[rows])
            weight = alpha * through
            behind = BACKGROUND * through[:, depth - 1 :] * (1.0 - alpha[:, depth - 1 :])
            goal = goal_s[rows]
            slope = jnp.zeros_like(weight)
            out, error = [], jnp.zeros_like(behind)
            for c in range(3):
                shown = jnp.sum(weight * colors[c], axis=1, keepdims=True) + behind
                image_s[rows, c : c + 1] = shown
                gap = shown - goal[:, c : c + 1]
                error = error + gap
                slope = slope + gap * colors[c]
                out.append(sums[c] + gap * weight)
            tail_s[rows, 0:1] = behind * error
            weight_s[rows] = through * slope
            for n, piece in enumerate(parts(weight * slope)):
                split_s[n, rows] = piece
            return tuple(out)

        zero = jnp.zeros((SIDE, depth), F32)
        color_grads.append(lax.fori_loop(0, pix // SIDE, shade, (zero, zero, zero)))
    later = one_hot(iota((depth, depth), 0) > iota((depth, depth), 1))
    run_s[...] = sum(dot(split_s[n], later) for n in range(3))
    entry_s[...] = jnp.zeros_like(entry_s)
    for t in range(tiles):
        u, v, conic_a, conic_b, conic_c, opacity = rows_of[t][:6]
        delta_u = deltas[t]

        def backward(i, sums, t=t, v=v):
            rows = chunk(t, i)
            alpha = alpha_s[rows]
            slope = weight_s[rows] - (run_s[rows] + tail_s[rows, 0:1]) / (1.0 - alpha)
            pull = alpha * slope
            delta_v = (i.astype(F32) - 7.5) - v
            pull_v = pull * delta_v
            return sums[0] + pull, sums[1] + pull_v, sums[2] + pull_v * delta_v

        zero = jnp.zeros((SIDE, depth), F32)
        plain, with_v, with_vv = lax.fori_loop(0, pix // SIDE, backward, (zero, zero, zero))

        def over(a):
            return jnp.sum(a, axis=0, keepdims=True)

        s_u, s_v = over(plain * delta_u), over(with_v)
        cols = slice(t * depth, (t + 1) * depth)
        entry_s[0:1, cols] = conic_a * s_u + conic_b * s_v
        entry_s[1:2, cols] = conic_b * s_u + conic_c * s_v
        entry_s[2:3, cols] = -0.5 * over(plain * delta_u * delta_u)
        entry_s[3:4, cols] = -over(with_v * delta_u)
        entry_s[4:5, cols] = -0.5 * over(with_vv)
        entry_s[5:6, cols] = over(plain) / opacity
        for c in range(3):
            entry_s[6 + c : 7 + c, cols] = over(color_grads[t][c])
        image_ref[t] = jnp.transpose(image_s[t * pix : (t + 1) * pix, 0:8])[0:3]
    grads = entry_s[...]
    slots = jnp.concatenate([jnp.where(rank == j, grads, 0.0) for j in range(CAP)], axis=0)
    sent = sum(dot_t(piece, named) for piece in parts(slots))
    grad_ref[:, :128] = jnp.transpose(sent[:128])
    grad_ref[:, 128:] = jnp.transpose(sent[128:])


def pullback_body(grad_ref, request_ref, params_ref, camera_ref, out_ref):
    gauss = params_ref.shape[1]
    cam = [camera_ref[0, i] for i in range(8)]
    hot = asked_hot(request_ref, gauss)
    came = jnp.concatenate(
        [jnp.transpose(grad_ref[:, :128]), jnp.transpose(grad_ref[:, 128:])], axis=0
    )
    came = jnp.concatenate([came[j * ROWS : (j + 1) * ROWS] for j in range(CAP)], axis=1)
    total = dot_t(jnp.concatenate(parts(came), axis=0), hot)
    total = total[:ROWS] + total[ROWS : 2 * ROWS] + total[2 * ROWS :]
    g_u, g_v, g_a, g_b, g_c = [total[r : r + 1] for r in range(5)]
    conic_a, conic_c, skew, root = conics(params_ref)
    half_b = g_b * (0.45 * skew * root)
    out_ref[0:1] = cam[0] * g_u + cam[4] * g_v
    out_ref[1:2] = cam[1] * g_u + cam[5] * g_v
    out_ref[2:3] = cam[2] * g_u + cam[6] * g_v
    out_ref[3:4] = g_a * conic_a + half_b
    out_ref[4:5] = g_b * 0.9 * (1.0 - skew * skew) * root
    out_ref[5:6] = g_c * conic_c + half_b
    level = sigmoid(params_ref[6:10])
    out_ref[6:10] = total[5:9] * level * (1.0 - level)


def adam_body(grads_ref, params_ref, moment1_ref, moment2_ref, rehome_ref, out_ref, stack_s):
    gauss = params_ref.shape[1]
    devices = out_ref.shape[0]
    sub = gauss // devices
    grad = (grads_ref[0] + grads_ref[1]) + (grads_ref[2] + grads_ref[3])
    moment1 = 0.9 * moment1_ref[...] + 0.1 * grad
    moment2 = 0.99 * moment2_ref[...] + 0.01 * grad * grad
    stack_s[...] = jnp.zeros_like(stack_s)
    stack_s[0:10] = params_ref[...] - 0.01 * moment1 / (jnp.sqrt(moment2) + 1e-08)
    stack_s[10:20] = moment1
    stack_s[20:30] = moment2
    block_of = iota((devices, gauss), 1) // sub == iota((devices, gauss), 0)
    homes = jnp.broadcast_to(rehome_ref[...].astype(F32), (8, devices)).astype(BF16)
    homes = dot(homes, one_hot(block_of))[0:1].astype(jnp.int32)
    place = iota((devices, gauss), 0) == homes
    within = iota((devices, gauss), 1) % sub
    pick = jnp.concatenate([one_hot(place & (within == i)) for i in range(sub)], axis=0)
    moved = dot_t(jnp.concatenate(parts(stack_s[...]), axis=0), pick)
    moved = moved[:32] + moved[32:64] + moved[64:]
    moved = jnp.concatenate(
        [moved[:, i * devices : (i + 1) * devices] for i in range(sub)], axis=0
    )
    out_ref[...] = jnp.transpose(moved)


def place_body(came_ref, params_ref, moment1_ref, moment2_ref):
    gauss = params_ref.shape[1]
    devices = came_ref.shape[0]
    sub = gauss // devices
    came = jnp.transpose(came_ref[...])
    came = jnp.concatenate([came[i * 32 : (i + 1) * 32] for i in range(sub)], axis=1)
    row = iota((gauss, gauss), 0)
    spot = one_hot(row % devices * sub + row // devices == iota((gauss, gauss), 1))
    out = dot(jnp.concatenate(parts(came), axis=0), spot)
    out = out[:32] + out[32:64] + out[64:]
    params_ref[...] = out[0:10]
    moment1_ref[...] = out[10:20]
    moment2_ref[...] = out[20:30]


def shape(*dims, dtype=F32):
    return jax.ShapeDtypeStruct(dims, dtype)


def exchange(x, axis="dev"):
    devices = lax.axis_size(axis)
    parcel = x.reshape(devices, -1, 128)
    return lax.all_to_all(parcel, axis, 0, 0, tiled=True).reshape(x.shape)


def local(params, moment1, moment2, camera, owner, local_index, target, rehome):
    devices = lax.axis_size("dev")
    reps = lax.axis_size("rep")
    gauss = params.shape[1]
    _, tiles, depth = local_index.shape
    entries = tiles * depth
    pix = target.shape[3]
    owners = owner.reshape(1, entries)
    ids = local_index.reshape(1, entries)
    request, rank = call(
        request_body, (shape(devices, 128), shape(1, entries, dtype=jnp.int32))
    )(owners, ids)
    request = exchange(request)
    response = call(
        respond_body, shape(devices, 256), [pltpu.VMEM((ROWS, gauss), F32)], smem=(2,)
    )(request, params, camera)
    response = exchange(response)
    plane = pltpu.VMEM((tiles * pix, depth), F32)
    column = pltpu.VMEM((tiles * pix, 128), F32)
    images, grads = call(
        composite_body,
        (shape(tiles, 3, pix), shape(devices, 256)),
        [
            plane, plane, plane, pltpu.VMEM((3, tiles * pix, depth), BF16),
            column, column, column, pltpu.VMEM((ROWS, entries), F32),
        ],
    )(response, owners, rank, target[0])
    grads = exchange(grads)
    grads = call(pullback_body, shape(10, gauss), smem=(3,))(grads, request, params, camera)
    grads = lax.all_to_all(
        jnp.broadcast_to(grads[None], (reps, 10, gauss)), "rep", 0, 0, tiled=True
    )
    moved = call(adam_body, shape(devices, 128), [pltpu.VMEM((32, gauss), F32)])(
        grads, params, moment1, moment2, rehome
    )
    moved = exchange(moved)
    out = call(place_body, (shape(10, gauss),) * 3)(moved)
    return (*out, images[None])


def solution(mesh):
    in_specs = (
        P(None, "dev"),
        P(None, "dev"),
        P(None, "dev"),
        P("rep", None),
        P("rep", "dev", None, None),
        P("rep", "dev", None),
        P("rep", "dev", None, None),
        P("dev", None),
    )
    out_specs = (P(None, "dev"), P(None, "dev"), P(None, "dev"), P("rep", "dev", None, None))
    return jax.shard_map(local, mesh=mesh, in_specs=in_specs, out_specs=out_specs, check_vma=False)
```

time: 471 us -> 117 us (0.25)
  waiting for transfers between devices: 307 us -> 23.8 us
  local copies, waits for them, and re-layouts: 63.2 us -> 2.81 us
  other arithmetic: 46.4 us -> 0 us
  blocking collectives: 13.2 us -> 56.2 us
  Pallas kernels: 0 us -> 20.1 us
  between operations: 14.6 us -> 0.76 us
  starting transfers between devices: 18.7 us -> 12.7 us
  matrix products: 5.91 us -> 0 us
    reduce_scatter x1 -> x0, waiting for transfers between devices: 193 us -> none  [local(): lax.psum_scatter(spread, 'dev', scatter_dimension=1, tiled=True)]
    all_gather x1 -> x0, waiting for transfers between devices: 88.6 us -> none  [local(): whole = lax.all_gather(projected, 'dev', axis=1, tiled=True)]
    all_to_all x0 -> x3, blocking collectives: none -> 56.2 us  [the longest x2 47.4 us: exchange(): return lax.all_to_all(parcel, axis, 0, 0, tiled=True).reshape(x.shape)]
    pallas_call x0 -> x6, Pallas kernels: none -> 20.1 us  [run(): pl.pallas_call(body, out_shape=out_shape, in_specs=specs, out_specs=outs,...]
    scatter-add x1 -> x0, local copies, waits for them, and re-layouts: 19.4 us -> none  [local(): jnp.zeros((9, gauss_dev * devices), jnp.float32).at[:, global_ids]]
    scatter-add x1 -> x0, other arithmetic: 19.2 us -> none  [local(): jnp.zeros((9, gauss_dev * devices), jnp.float32).at[:, global_ids]]
    all_gather x1 -> x0, local copies, waits for them, and re-layouts: 16.9 us -> none  [local(): whole = lax.all_gather(projected, 'dev', axis=1, tiled=True)]
    gather x3 -> x0, local copies, waits for them, and re-layouts: 14.7 us -> none  [the longest x2 13.5 us: local(): entries = jnp.take(whole, global_ids, axis=1)]
  transfers between devices with their start and end apart: 3 -> 2, of which waited for: 3 -> 2; matrix products, arithmetic and copies ran while one was open for 1% -> 1% of each run, Pallas kernels for 0% -> 0%
where the time goes in v1:
time: 117 us; the launch traced here: 116 us
  blocking collectives  56.2 us (48%)
  waiting for transfers between devices  23.8 us (20%)
  Pallas kernels  20.1 us (17%)
  starting transfers between devices  12.7 us (11%)
  local copies, waits for them, and re-layouts  2.81 us (2%)
    all_to_all x2, blocking collectives, exchange(): return lax.all_to_all(parcel, axis, 0, 0, tiled=True).reshape(x.shape)  47.4 us
    all_to_all x2, waiting for transfers between devices, exchange(): return lax.all_to_all(parcel, axis, 0, 0, tiled=True).reshape(x.shape)  23.8 us
    pallas_call x6, Pallas kernels, run(): pl.pallas_call(body, out_shape=out_shape, in_specs=specs, out_specs=outs,...  20.1 us
    all_to_all x2, starting transfers between devices, exchange(): return lax.all_to_all(parcel, axis, 0, 0, tiled=True).reshape(x.shape)  12.7 us
    all_to_all x1, blocking collectives, local(): lax.all_to_all(jnp.broadcast_to(grads[None], (reps, 10, gauss)), 'rep', 0...  8.77 us
  transfers between devices with their start and end apart: 2, of which 2 were waited for; matrix products, arithmetic and copies ran while one was open for 1% of the time, Pallas kernels for 0%

profile of v1, /device:TPU:1, one launch (start us, length us, event | category | flops | bytes accessed | tf_op | source)
XLA Modules:
  0.0 116.4 jit_solution(1602008818825540344)
XLA Ops:
  0.6 0.0 copy-start.3
  0.6 0.7 copy.18
  1.3 0.0 copy-done.3
  1.3 0.7 shard_map.111
  2.1 0.0 copy-start
  2.1 29.7 %all_to_all.25 = f32[128,1,128]{2,1,0:T(1,128)S(1)} all-to-all(f32[128,1,128]{2,1,0:T(1,128)S(1)} %bitcast.28), channel_id=1, replica_groups=mesh['dev'=128,'rep'=4] {'dev'}, dimensions={0} | all-to-all | bytes 131072 | tf_op jit(solution)/shard_map/all_to_all | solution.py:323
  31.8 0.0 copy-start.4
  31.8 0.0 copy-done
  31.8 0.7 copy-done.4
  32.4 1.1 shard_map.112
  33.6 0.7 reshape.43
  34.3 0.0 copy-start.6
  34.3 5.8 %all-to-all-start.1 = ((f32[128,2,128]{2,1,0:T(2,128)}), f32[128,2,128]{2,1,0:T(2,128)S(1)}, u32[]{:S(2)}, u32[]{:S(2)}) async-start(f32[128,2,128]{2,1,0:T(2,128)} %reshape.43), calls=%async_computation.1 | async-start | bytes 262144 | tf_op jit(solution)/shard_map/all_to_all | solution.py:323
  40.1 0.0 copy-done.6
  40.1 12.8 %all-to-all-done.1 = f32[128,2,128]{2,1,0:T(2,128)S(1)} async-done(((f32[128,2,128]{2,1,0:T(2,128)}), f32[128,2,128]{2,1,0:T(2,128)S(1)}, u32[]{:S(2)}, u32[]{:S(2)}) %all-to-all-start.1) | async-done | bytes 131104 | tf_op jit(solution)/shard_map/all_to_all | solution.py:323
  53.0 14.8 %shard_map.113 = (f32[2,3,256]{2,1,0:T(4,128)S(1)}, f32[128,256]{1,0:T(8,128)S(1)}) custom-call(f32[128,256]{1,0:T(8,128)S(1)} %bitcast.25, s32[1,1024]{1,0:T(1,128)S(1)} %bitcast.31, s32[1,1024]{1,0:T(1,128)S(1)} %get-tuple-element.12.rank_ref, f32[2,3,256]{2,1,0:T(4,128)S(1)} %bitcast.29), custom_call_target="tpu_custom_call" | custom-call | tf_op jit(solution)/shard_map/pallas_call | solution.py:51
  67.7 0.1 reshape.45
  67.8 17.8 %all_to_all.26 = f32[128,2,128]{2,1,0:T(2,128)S(1)} all-to-all(f32[128,2,128]{2,1,0:T(2,128)S(1)} %reshape.45), channel_id=1, replica_groups=mesh['dev'=128,'rep'=4] {'dev'}, dimensions={0} | all-to-all | bytes 262144 | tf_op jit(solution)/shard_map/all_to_all | solution.py:323
  85.6 1.4 %shard_map.114 = f32[10,512]{1,0:T(8,128)S(1)} custom-call(f32[128,256]{1,0:T(8,128)S(1)} %bitcast.26, f32[128,128]{1,0:T(8,128)S(1)} %bitcast.24, f32[10,512]{1,0:T(8,128)S(1)} %copy-done, f32[1,8]{1,0:T(1,128)S(1)} %copy-done.4), custom_call_target="tpu_custom_call" | custom-call | tf_op jit(solution)/shard_map/pallas_call | solution.py:51
  87.0 0.0 copy-start.1
  87.0 0.0 copy-start.2
  87.0 0.0 copy-start.5
  87.0 8.8 %all_to_all.27.grads_ref = f32[4,10,512]{2,1,0:T(8,128)S(1)} all-to-all(f32[4,10,512]{2,1,0:T(8,128)S(1)} %broadcast_in_dim.4), channel_id=1, replica_groups=mesh['dev'=128,'rep'=4] {'rep'}, dimensions={0} | all-to-all | bytes 163840 | tf_op jit(solution)/shard_map/all_to_all | solution.py:355
  95.8 0.0 copy-done.1
  95.8 0.0 copy-done.2
  95.8 0.0 copy-done.5
  95.8 1.2 %shard_map.115 = f32[128,128]{1,0:T(8,128)} custom-call(f32[4,10,512]{2,1,0:T(8,128)S(1)} %all_to_all.27.grads_ref, f32[10,512]{1,0:T(8,128)S(1)} %copy-done, f32[10,512]{1,0:T(8,128)S(1)} %copy-done.1, f32[10,512]{1,0:T(8,128)S(1)} %copy-done.2, s32[1,128]{1,0:T(1,128)S(1)} %copy-done.5), custom_call_target="tpu_custom_call" | custom-call | tf_op jit(solution)/shard_map/pallas_call | solution.py:51
  97.0 6.9 %all-to-all-start.4 = ((f32[128,1,128]{2,1,0:T(1,128)}), f32[128,1,128]{2,1,0:T(1,128)S(1)}, u32[]{:S(2)}, u32[]{:S(2)}) async-start(f32[128,1,128]{2,1,0:T(1,128)} %bitcast.6), calls=%async_computation.4 | async-start | bytes 131072 | tf_op jit(solution)/shard_map/all_to_all | solution.py:323
  103.9 0.6 copy.17
  104.5 11.0 %all-to-all-done.4 = f32[128,1,128]{2,1,0:T(1,128)S(1)} async-done(((f32[128,1,128]{2,1,0:T(1,128)}), f32[128,1,128]{2,1,0:T(1,128)S(1)}, u32[]{:S(2)}, u32[]{:S(2)}) %all-to-all-start.4) | async-done | bytes 65568 | tf_op jit(solution)/shard_map/all_to_all | solution.py:323
  115.4 0.9 shard_map.116
  (4 shorter events, 0.0 us)
Async XLA Ops:
  0.6 0.7 copy-start.3
  2.1 29.7 %copy-start = (f32[10,512]{1,0:T(8,128)S(1)}, f32[10,512]{1,0:T(8,128)}, u32[]{:S(2)}) copy-start(f32[10,512]{1,0:T(8,128)} %params_ref.5) | copy-start | bytes 61444
  31.8 0.7 copy-start.4
  34.3 5.8 %copy-start.6 = (f32[1,2,3,256]{3,1,2,0:T(2,128)S(1)}, f32[1,2,3,256]{3,1,2,0:T(2,128)}, u32[]{:S(2)}) copy-start(f32[1,2,3,256]{3,1,2,0:T(2,128)} %param.14) | copy-start | bytes 18436
  34.3 18.7 %all-to-all-start.1 = ((f32[128,2,128]{2,1,0:T(2,128)}), f32[128,2,128]{2,1,0:T(2,128)S(1)}, u32[]{:S(2)}, u32[]{:S(2)}) async-start(f32[128,2,128]{2,1,0:T(2,128)} %reshape.43), calls=%async_computation.1 | async-start | bytes 262144 | tf_op jit(solution)/shard_map/all_to_all | solution.py:323
  87.0 8.8 %copy-start.1 = (f32[10,512]{1,0:T(8,128)S(1)}, f32[10,512]{1,0:T(8,128)}, u32[]{:S(2)}) copy-start(f32[10,512]{1,0:T(8,128)} %moment1_ref.1) | copy-start | bytes 61444
  87.0 8.8 %copy-start.2 = (f32[10,512]{1,0:T(8,128)S(1)}, f32[10,512]{1,0:T(8,128)}, u32[]{:S(2)}) copy-start(f32[10,512]{1,0:T(8,128)} %moment2_ref.1) | copy-start | bytes 61444
  87.0 8.8 %copy-start.5 = (s32[1,128]{1,0:T(1,128)S(1)}, s32[1,128]{1,0:T(1,128)}, u32[]{:S(2)}) copy-start(s32[1,128]{1,0:T(1,128)} %rehome_ref.1) | copy-start | bytes 1540
  97.0 18.5 %all-to-all-start.4 = ((f32[128,1,128]{2,1,0:T(1,128)}), f32[128,1,128]{2,1,0:T(1,128)S(1)}, u32[]{:S(2)}, u32[]{:S(2)}) async-start(f32[128,1,128]{2,1,0:T(1,128)} %bitcast.6), calls=%async_computation.4 | async-start | bytes 131072 | tf_op jit(solution)/shard_map/all_to_all | solution.py:323

commit v2 on v0

v2 whole, which is shorter than its diff:
```python
import functools

import jax
import jax.numpy as jnp
from jax import lax
from jax.experimental import pallas as pl
from jax.experimental.pallas import tpu as pltpu
from jax.sharding import PartitionSpec as P

SIDE = 16
BACKGROUND = 0.5
CAP = 16
SUB = 4
HOME_CAP = 32
UNROLL = 4
ROWS = 16
VMEM = 48 * 1024 * 1024
F32 = jnp.float32
BF16 = jnp.bfloat16


def one_hot(condition):
    return jnp.where(condition, 1.0, 0.0).astype(BF16)


def parts(x, count=3):
    out = []
    for _ in range(count):
        piece = x.astype(BF16)
        out.append(piece)
        x = x - piece.astype(F32)
    return out


def iota(shape, dim):
    return lax.broadcasted_iota(jnp.int32, shape, dim)


def dot(a, b):
    return lax.dot_general(a, b, (((1,), (0,)), ((), ())), preferred_element_type=F32)


def dot_t(a, b):
    return lax.dot_general(a, b, (((1,), (1,)), ((), ())), preferred_element_type=F32)


def call(body, out_shape, scratch=(), smem=()):
    def run(*args):
        specs = [
            pl.BlockSpec(memory_space=pltpu.SMEM if i in smem else pltpu.VMEM)
            for i in range(len(args))
        ]
        outs = jax.tree.map(lambda _: pl.BlockSpec(memory_space=pltpu.VMEM), out_shape)
        return pl.pallas_call(
            body,
            out_shape=out_shape,
            in_specs=specs,
            out_specs=outs,
            scratch_shapes=list(scratch),
            compiler_params=pltpu.CompilerParams(vmem_limit_bytes=VMEM),
        )(*args)

    return run


def along(ref):
    return jnp.concatenate([ref[t : t + 1] for t in range(ref.shape[0])], axis=1)


def rank_of(device, devices):
    entries = device.shape[1]
    step = 256
    before = one_hot(iota((step, step), 0) < iota((step, step), 1))
    base = jnp.zeros((devices, 1), F32)
    ranks, hots = [], []
    for start in range(0, entries, step):
        named = jnp.where(
            iota((devices, step), 0) == device[:, start : start + step], 1.0, 0.0
        )
        hots.append(named.astype(BF16))
        count = dot(hots[-1], before) + base
        base = base + jnp.sum(named, axis=1, keepdims=True)
        ranks.append(jnp.sum(named * count, axis=0, keepdims=True).astype(jnp.int32))
    return jnp.concatenate(ranks, axis=1), jnp.concatenate(hots, axis=1)


def homes_of(rehome_ref, gauss):
    devices = rehome_ref.shape[1]
    sub = gauss // devices
    homes = jnp.broadcast_to(rehome_ref[...].astype(F32), (8, devices)).astype(BF16)
    return dot(homes, one_hot(iota((devices, gauss), 1) // sub == iota((devices, gauss), 0)))[0:1]


def pack_blocks(stack, homes, devices):
    gauss = stack.shape[1]
    sub = gauss // devices
    place = iota((devices, gauss), 0) == homes.astype(jnp.int32)
    within = iota((devices, gauss), 1) % sub
    pick = jnp.concatenate([one_hot(place & (within == i)) for i in range(sub)], axis=0)
    moved = dot_t(jnp.concatenate(parts(stack), axis=0), pick)
    moved = moved[:32] + moved[32:64] + moved[64:]
    return jnp.transpose(
        jnp.concatenate([moved[:, i * devices : (i + 1) * devices] for i in range(sub)], axis=0)
    )


def place_blocks(came, gauss):
    devices = came.shape[0]
    sub = gauss // devices
    came = jnp.transpose(came)
    came = jnp.concatenate([came[i * 32 : (i + 1) * 32] for i in range(sub)], axis=1)
    row = iota((gauss, gauss), 0)
    spot = one_hot(row % devices * sub + row // devices == iota((gauss, gauss), 1))
    out = dot(jnp.concatenate(parts(came), axis=0), spot)
    return out[:32] + out[32:64] + out[64:]


def request_body(
    owner_ref, index_ref, params_ref, moment1_ref, moment2_ref, rehome_ref,
    request_ref, rank_ref, stack_s,
):
    gauss = params_ref.shape[1]
    devices = request_ref.shape[0]
    rank, named = rank_of(owner_ref[...], devices)
    rank_ref[...] = rank
    ids = along(index_ref)
    slot = iota((CAP, ids.shape[1]), 0) == rank
    high = jnp.where(slot, (ids >> 4).astype(F32), 0.0)
    low = jnp.where(slot, (ids & 15).astype(F32), 0.0)
    total = dot_t(named, jnp.concatenate([high, low], axis=0).astype(BF16))
    ids = 16.0 * total[:, :CAP] + total[:, CAP:]
    stack_s[...] = jnp.zeros_like(stack_s)
    stack_s[0:10] = params_ref[...]
    stack_s[10:20] = moment1_ref[...]
    stack_s[20:30] = moment2_ref[...]
    request_ref[:, 0:128] = pack_blocks(stack_s[...], homes_of(rehome_ref, gauss), devices)
    request_ref[:, 128:256] = jnp.concatenate([ids, jnp.zeros((devices, 128 - CAP), F32)], axis=1)


def asked_hot(request_ref, gauss):
    devices = request_ref.shape[0]
    ids = jnp.transpose(request_ref[:, 128:256]).astype(jnp.int32)
    return jnp.concatenate(
        [one_hot(iota((gauss, devices), 0) == ids[j : j + 1]) for j in range(CAP)], axis=1
    )


def respond_body(request_ref, params_ref, rehome_ref, response_ref, table):
    gauss = params_ref.shape[1]
    devices = request_ref.shape[0]
    table[...] = jnp.zeros_like(table)
    table[0:10] = params_ref[...]
    table[10:11] = homes_of(rehome_ref, gauss)
    got = dot(jnp.concatenate(parts(table[...]), axis=0), asked_hot(request_ref, gauss))
    got = got[:ROWS] + got[ROWS : 2 * ROWS] + got[2 * ROWS :]
    for half in range(2):
        block = jnp.concatenate(
            [got[:, j * devices : (j + 1) * devices] for j in range(half * 8, half * 8 + 8)],
            axis=0,
        )
        response_ref[:, half * 128 : half * 128 + 128] = jnp.transpose(block)


def sigmoid(x):
    return 1.0 / (1.0 + jnp.exp(-x))


def stacked(pieces):
    rows = [piece.astype(F32) for piece in pieces]
    return jnp.concatenate([*rows, jnp.zeros_like(rows[0])], axis=0).astype(BF16)


def groups(x):
    return x[0:8] + x[8:16] + x[16:24]


def composite_body(
    response_ref, owner_ref, index_ref, rank_ref, target_ref, camera_ref,
    image_ref, grad_ref, entry_ref,
    alpha_s, run_s, slope_s, split_s, entry_s,
):
    devices = response_ref.shape[0]
    entries = owner_ref.shape[1]
    _, tiles, pix = target_ref.shape
    depth = entries // tiles
    cam = [camera_ref[0, i] for i in range(8)]
    owner, rank = owner_ref[...], rank_ref[...]
    named = one_hot(iota((devices, entries), 0) == owner)
    got = jnp.concatenate(
        [jnp.transpose(response_ref[:, :128]), jnp.transpose(response_ref[:, 128:])], axis=0
    )
    spread = sum(dot(piece, named) for piece in parts(got))
    values = jnp.zeros((ROWS, entries), F32)
    for j in range(CAP):
        values = values + jnp.where(rank == j, spread[j * ROWS : (j + 1) * ROWS], 0.0)
    x, y, z = values[0:1], values[1:2], values[2:3]
    screen_u = cam[0] * x + cam[1] * y + cam[2] * z + cam[3]
    screen_v = cam[4] * x + cam[5] * y + cam[6] * z + cam[7]
    conic_a, conic_c, skew = jnp.exp(values[3:4]), jnp.exp(values[5:6]), jnp.tanh(values[4:5])
    root = jnp.sqrt(conic_a * conic_c)
    conic_b = 0.9 * skew * root
    level = sigmoid(values[0:16])
    opacity = level[6:7]
    entry_s[...] = jnp.zeros_like(entry_s)
    entry_s[0:3] = level[7:10]
    colors = entry_s[0:8]
    peak, half_a, half_c = 0.99 * opacity, -0.5 * conic_a, -0.5 * conic_c
    across = iota((SIDE, depth), 0).astype(F32) - 7.5

    def chunk(t, i):
        return pl.ds(pl.multiple_of(t * pix + i * SIDE, SIDE), SIDE)

    def of(t):
        return slice(t * depth, (t + 1) * depth)

    def over_rows(body, init, t):
        return lax.fori_loop(0, pix // SIDE, functools.partial(body, t), init, unroll=UNROLL)

    def save(rows, x):
        for n, piece in enumerate(parts(x, 2)):
            split_s[n, rows] = piece

    for t in range(tiles):
        delta_u = across - screen_u[:, of(t)]
        first = half_a[:, of(t)] * delta_u * delta_u
        mixed = -conic_b[:, of(t)] * delta_u

        def forward(t, i, carry, first=first, mixed=mixed):
            rows = chunk(t, i)
            delta_v = (i.astype(F32) - 7.5) - screen_v[:, of(t)]
            power = first + delta_v * (mixed + half_c[:, of(t)] * delta_v)
            alpha = peak[:, of(t)] * jnp.exp(power)
            alpha_s[rows] = alpha
            save(rows, jnp.log(1.0 - alpha))
            return carry

        over_rows(forward, 0, t)
    half = depth // 2
    tri = one_hot(iota((half, half), 0) < iota((half, half), 1))
    full = jnp.ones((half, half), BF16)
    run_s[:, :half] = dot(split_s[0, :, :half], tri) + dot(split_s[1, :, :half], tri)
    run_s[:, half:] = (
        dot(split_s[0, :, half:], tri) + dot(split_s[1, :, half:], tri)
        + dot(split_s[0, :, :half], full) + dot(split_s[1, :, :half], full)
    )
    ones = jnp.ones((16, depth), BF16)
    behind = dot_t(ones, split_s[0]) + dot_t(ones, split_s[1])
    behind = BACKGROUND * jnp.exp(behind[0:1])
    for t in range(tiles):

        def weigh(t, i, carry):
            rows = chunk(t, i)
            through = jnp.exp(run_s[rows])
            run_s[rows] = through
            save(rows, alpha_s[rows] * through)
            return carry

        over_rows(weigh, 0, t)
    color_grads, tails = [], []
    for t in range(tiles):
        px = slice(t * pix, (t + 1) * pix)
        paints = parts(colors[:, of(t)])
        paint = stacked(paints)
        shown = groups(dot_t(paint, split_s[0, px]) + dot_t(paint, split_s[1, px]))
        shown = shown + behind[:, px]
        gaps = []
        for c in range(3):
            image_ref[c, t : t + 1] = shown[c : c + 1]
            gaps.append(shown[c : c + 1] - target_ref[c, t : t + 1])
        tail = behind[:, px] * (gaps[0] + gaps[1] + gaps[2])
        gap = jnp.concatenate([*gaps, jnp.zeros((5, pix), F32)], axis=0)
        gap_parts = parts(gap)
        drawn = stacked(gap_parts)
        color_grads.append(groups(dot(drawn, split_s[0, px]) + dot(drawn, split_s[1, px])))
        high, middle, low = [piece.astype(F32) for piece in gap_parts]
        ends = [piece.astype(F32) for piece in parts(tail)]
        ends = jnp.concatenate([*ends, jnp.zeros((5, pix), F32)], axis=0)
        left = jnp.concatenate(
            [high, high, high, middle, middle, low, ends, jnp.zeros((72, pix), F32)], axis=0
        )
        left = jnp.concatenate(
            [jnp.transpose(left[:, :128]), jnp.transpose(left[:, 128:])], axis=0
        ).astype(BF16)
        high, middle, low = [piece.astype(F32) for piece in paints]
        right = jnp.concatenate(
            [high, middle, low, high, middle, high, jnp.zeros((80, depth), F32)], axis=0
        ).astype(BF16)
        slope_s[px] = dot(left, right)
        row = iota((128, depth), 0)
        tails.append(dot(left, one_hot((row >= 48) & (row < 51))))
    for t in range(tiles):

        def spread_back(t, i, carry):
            rows = chunk(t, i)
            through_slope = run_s[rows] * slope_s[rows]
            slope_s[rows] = through_slope
            save(rows, alpha_s[rows] * through_slope)
            return carry

        over_rows(spread_back, 0, t)
    tri = one_hot(iota((half, half), 0) > iota((half, half), 1))
    for t in range(tiles):
        px = slice(t * pix, (t + 1) * pix)
        run_s[px, half:] = (
            dot(split_s[0, px, half:], tri) + dot(split_s[1, px, half:], tri)
            + tails[t][:, half:]
        )
        run_s[px, :half] = (
            dot(split_s[0, px, :half], tri) + dot(split_s[1, px, :half], tri)
            + dot(split_s[0, px, half:], full) + dot(split_s[1, px, half:], full)
            + tails[t][:, :half]
        )
    sums = []
    for t in range(tiles):

        def backward(t, i, sums):
            rows = chunk(t, i)
            alpha = alpha_s[rows]
            pull = alpha * (slope_s[rows] - run_s[rows] / (1.0 - alpha))
            delta_v = (i.astype(F32) - 7.5) - screen_v[:, of(t)]
            pull_v = pull * delta_v
            return sums[0] + pull, sums[1] + pull_v, sums[2] + pull_v * delta_v

        zero = jnp.zeros((SIDE, depth), F32)
        plain, with_v, with_vv = over_rows(backward, (zero, zero, zero), t)
        delta_u = across - screen_u[:, of(t)]
        plain_u = plain * delta_u
        sums.append(
            [
                jnp.sum(a, axis=0, keepdims=True)
                for a in (plain, plain_u, with_v, plain_u * delta_u, with_v * delta_u, with_vv)
            ]
        )
    s_0, s_u, s_v, s_uu, s_uv, s_vv = [
        jnp.concatenate([s[n] for s in sums], axis=1) for n in range(6)
    ]
    g_u = conic_a * s_u + conic_b * s_v
    g_v = conic_b * s_u + conic_c * s_v
    half_b = -0.5 * s_uv * conic_b
    for c in range(3):
        entry_s[c : c + 1] = cam[c] * g_u + cam[4 + c] * g_v
    entry_s[3:4] = half_b - 0.5 * s_uu * conic_a
    entry_s[4:5] = -0.9 * s_uv * (1.0 - skew * skew) * root
    entry_s[5:6] = half_b - 0.5 * s_vv * conic_c
    entry_s[6:7] = s_0 * (1.0 - opacity)
    tint = jnp.concatenate(color_grads, axis=1)[0:3]
    entry_s[7:10] = tint * level[7:10] * (1.0 - level[7:10])
    entry_ref[...] = entry_s[...]
    home = (values[10:11] + 0.5).astype(jnp.int32)
    spot = owner * SUB + along(index_ref) % SUB
    entry_s[10:11] = spot.astype(F32)
    order, moves = rank_of(home, devices)
    slots = iota((HOME_CAP, entries), 0) == order
    grads = entry_s[...]
    sent = 0.0
    for piece in parts(grads, 2):
        piece = piece.astype(F32)
        rows = jnp.concatenate(
            [jnp.where(slots, piece[r : r + 1], 0.0).astype(BF16) for r in range(11)], axis=0
        )
        sent = sent + dot_t(rows, moves)
    over = jnp.max(order, axis=1, keepdims=True) >= HOME_CAP
    flag = jnp.where(over, 1.0, 0.0) + jnp.zeros((HOME_CAP, devices), F32)
    sent = jnp.concatenate([sent, flag], axis=0)
    for n in range(3):
        grad_ref[:, n * 128 : (n + 1) * 128] = jnp.transpose(sent[n * 128 : (n + 1) * 128])


def collect_body(grad_ref, out_ref, came_s):
    gauss = out_ref.shape[1]
    devices = grad_ref.shape[0]
    for n in range(3):
        came_s[n * 128 : (n + 1) * 128] = jnp.transpose(grad_ref[:, n * 128 : (n + 1) * 128])
    spots = (came_s[10 * HOME_CAP : 11 * HOME_CAP] + 0.5).astype(jnp.int32)
    total = jnp.zeros((2 * ROWS, gauss), F32)
    zero = jnp.zeros((6, devices), F32)
    for start in range(0, HOME_CAP, 8):
        hot, came = [], []
        for j in range(start, start + 8):
            hot.append(one_hot(iota((gauss, devices), 0) == spots[j : j + 1]))
            came.append(
                jnp.concatenate([came_s[pl.ds(j, 10, stride=HOME_CAP), :], zero], axis=0)
            )
        came = parts(jnp.concatenate(came, axis=1), 2)
        total = total + dot_t(jnp.concatenate(came, axis=0), jnp.concatenate(hot, axis=1))
    out_ref[...] = total[:ROWS] + total[ROWS:]
    flags = came_s[11 * HOME_CAP : 12 * HOME_CAP]
    flag = jnp.max(jnp.max(flags, axis=1, keepdims=True), axis=0, keepdims=True)
    out_ref[10:11] = flag + jnp.zeros((1, gauss), F32)


def to_owner_body(entry_ref, owner_ref, rank_ref, out_ref):
    devices = out_ref.shape[0]
    rank = rank_ref[...]
    named = one_hot(iota((devices, rank.shape[1]), 0) == owner_ref[...])
    grads = entry_ref[...]
    slots = jnp.concatenate([jnp.where(rank == j, grads, 0.0) for j in range(CAP)], axis=0)
    sent = sum(dot_t(piece, named) for piece in parts(slots))
    out_ref[:, :128] = jnp.transpose(sent[:128])
    out_ref[:, 128:] = jnp.transpose(sent[128:])


def at_owner_body(grad_ref, request_ref, rehome_ref, out_ref, *, gauss):
    devices = grad_ref.shape[0]
    came = jnp.concatenate(
        [jnp.transpose(grad_ref[:, :128]), jnp.transpose(grad_ref[:, 128:])], axis=0
    )
    came = jnp.concatenate([came[j * ROWS : (j + 1) * ROWS] for j in range(CAP)], axis=1)
    total = dot_t(jnp.concatenate(parts(came), axis=0), asked_hot(request_ref, gauss))
    total = total[:ROWS] + total[ROWS : 2 * ROWS] + total[2 * ROWS :]
    stack = jnp.concatenate([total, jnp.zeros_like(total)], axis=0)
    out_ref[...] = pack_blocks(stack, homes_of(rehome_ref, gauss), devices)


def at_home_body(came_ref, out_ref):
    out_ref[...] = place_blocks(came_ref[...], out_ref.shape[1])[:ROWS]


def adam_body(grads_ref, request_ref, params_ref, moment1_ref, moment2_ref):
    old = place_blocks(request_ref[:, 0:128], params_ref.shape[1])
    grad = (grads_ref[0] + grads_ref[1]) + (grads_ref[2] + grads_ref[3])
    grad = grad[0:10]
    moment1 = 0.9 * old[10:20] + 0.1 * grad
    moment2 = 0.99 * old[20:30] + 0.01 * grad * grad
    params_ref[...] = old[0:10] - 0.01 * moment1 / (jnp.sqrt(moment2) + 1e-08)
    moment1_ref[...] = moment1
    moment2_ref[...] = moment2


def shape(*dims, dtype=F32):
    return jax.ShapeDtypeStruct(dims, dtype)


def exchange(x):
    devices = lax.axis_size("dev")
    parcel = x.reshape(devices, -1, 128)
    return lax.all_to_all(parcel, "dev", 0, 0, tiled=True).reshape(x.shape)


def share(x):
    copies = jnp.broadcast_to(x[None], (lax.axis_size("rep"), *x.shape))
    return lax.all_to_all(copies, "rep", 0, 0, tiled=True)


def local(params, moment1, moment2, camera, owner, local_index, target, rehome):
    devices = lax.axis_size("dev")
    gauss = params.shape[1]
    _, tiles, depth = local_index.shape
    entries = tiles * depth
    pix = target.shape[3]
    owners = owner.reshape(1, entries)
    ids = local_index[0]
    request, rank = call(
        request_body,
        (shape(devices, 256), shape(1, entries, dtype=jnp.int32)),
        [pltpu.VMEM((32, gauss), F32)],
    )(owners, ids, params, moment1, moment2, rehome)
    request = exchange(request)
    response = call(respond_body, shape(devices, 256), [pltpu.VMEM((ROWS, gauss), F32)])(
        request, params, rehome
    )
    response = exchange(response)
    plane = pltpu.VMEM((tiles * pix, depth), F32)
    images, grads, by_entry = call(
        composite_body,
        (shape(3, tiles, pix), shape(devices, 384), shape(ROWS, entries)),
        [
            plane, plane, plane, pltpu.VMEM((2, tiles * pix, depth), BF16),
            pltpu.VMEM((ROWS, entries), F32),
        ],
        smem=(5,),
    )(response, owners, ids, rank, target[0].transpose(1, 0, 2), camera)
    grads = exchange(grads)
    grads = call(collect_body, shape(ROWS, gauss), [pltpu.VMEM((384, devices), F32)])(grads)
    grads = share(grads)

    def by_owner(grads, by_entry, owners, rank, request, rehome):
        sent = call(to_owner_body, shape(devices, 256))(by_entry, owners, rank)
        sent = call(functools.partial(at_owner_body, gauss=gauss), shape(devices, 128))(
            exchange(sent), request, rehome
        )
        return share(call(at_home_body, shape(ROWS, gauss))(exchange(sent)))

    full = jnp.max(grads[:, 10, 0]) > 0.5
    grads = lax.cond(
        full, by_owner, lambda grads, *rest: grads, grads, by_entry, owners, rank, request, rehome
    )
    out = call(adam_body, (shape(10, gauss),) * 3)(grads, request)
    return (*out, images.transpose(1, 0, 2)[None])


def solution(mesh):
    in_specs = (
        P(None, "dev"),
        P(None, "dev"),
        P(None, "dev"),
        P("rep", None),
        P("rep", "dev", None, None),
        P("rep", "dev", None),
        P("rep", "dev", None, None),
        P("dev", None),
    )
    out_specs = (P(None, "dev"), P(None, "dev"), P(None, "dev"), P("rep", "dev", None, None))
    return jax.shard_map(local, mesh=mesh, in_specs=in_specs, out_specs=out_specs, check_vma=False)
```

time: 471 us -> 98.9 us (0.21)
  waiting for transfers between devices: 307 us -> 4.83 us
  local copies, waits for them, and re-layouts: 63.2 us -> 6.42 us
  blocking collectives: 13.2 us -> 69 us
  other arithmetic: 46.4 us -> 0.6 us
  starting transfers between devices: 18.7 us -> 4.03 us
  between operations: 14.6 us -> 1.4 us
  Pallas kernels: 0 us -> 11.7 us
  matrix products: 5.91 us -> 0 us
    reduce_scatter x1 -> x0, waiting for transfers between devices: 193 us -> none  [local(): lax.psum_scatter(spread, 'dev', scatter_dimension=1, tiled=True)]
    all_gather x1 -> x0, waiting for transfers between devices: 88.6 us -> none  [local(): whole = lax.all_gather(projected, 'dev', axis=1, tiled=True)]
    all_to_all x0 -> x3, blocking collectives: none -> 69 us  [exchange(): return lax.all_to_all(parcel, 'dev', 0, 0, tiled=True).reshape(x.shape)]
    all_to_all x1, waiting for transfers between devices: 25.3 us -> 4.83 us  [share(): return lax.all_to_all(copies, 'rep', 0, 0, tiled=True)]
    scatter-add x1 -> x0, local copies, waits for them, and re-layouts: 19.4 us -> none  [local(): jnp.zeros((9, gauss_dev * devices), jnp.float32).at[:, global_ids]]
    scatter-add x1 -> x0, other arithmetic: 19.2 us -> none  [local(): jnp.zeros((9, gauss_dev * devices), jnp.float32).at[:, global_ids]]
    all_gather x1 -> x0, local copies, waits for them, and re-layouts: 16.9 us -> none  [local(): whole = lax.all_gather(projected, 'dev', axis=1, tiled=True)]
    gather x3 -> x0, local copies, waits for them, and re-layouts: 14.7 us -> none  [the longest x2 13.5 us: local(): entries = jnp.take(whole, global_ids, axis=1)]
  transfers between devices with their start and end apart: 3 -> 1, of which waited for: 3 -> 1; matrix products, arithmetic and copies ran while one was open for 1% -> 0% of each run, Pallas kernels for 0% -> 0%
where the time goes in v2:
time: 98.9 us; the launch traced here: 98.1 us
  blocking collectives  69 us (70%)
  Pallas kernels  11.7 us (12%)
  local copies, waits for them, and re-layouts  6.42 us (6%)
  waiting for transfers between devices  4.83 us (5%)
  starting transfers between devices  4.03 us (4%)
  between operations  1.4 us (1%)
    all_to_all x3, blocking collectives, exchange(): return lax.all_to_all(parcel, 'dev', 0, 0, tiled=True).reshape(x.shape)  69 us
    pallas_call x5, Pallas kernels, run(): pl.pallas_call(body, out_shape=out_shape, in_specs=specs, out_specs=outs,...  11.7 us
    unnamed x22, local copies, waits for them, and re-layouts  5.06 us
    all_to_all x1, waiting for transfers between devices, share(): return lax.all_to_all(copies, 'rep', 0, 0, tiled=True)  4.83 us
    all_to_all x1, starting transfers between devices, share(): return lax.all_to_all(copies, 'rep', 0, 0, tiled=True)  4.03 us
  transfers between devices with their start and end apart: 1, of which 1 were waited for; matrix products, arithmetic and copies ran while one was open for 0% of the time, Pallas kernels for 0%

profile of v2, /device:TPU:1, one launch (start us, length us, event | category | flops | bytes accessed | tf_op | source)
XLA Modules:
  0.0 98.1 jit_solution(6055616696745103358)
XLA Ops:
  0.6 0.0 copy-start.9
  0.6 0.6 copy-done.9
  1.3 0.0 copy-start
  1.3 0.8 copy-done
  2.0 0.0 copy-start.2
  2.0 0.8 copy-done.2
  2.8 0.0 copy-start.3
  2.8 0.8 copy-done.3
  3.6 0.0 copy-start.4
  3.6 0.7 copy-done.4
  4.3 1.4 %shard_map.111 = (f32[128,256]{1,0:T(8,128)S(1)}, s32[1,1024]{1,0:T(1,128)S(1)}) custom-call(s32[1,1024]{1,0:T(1,128)} %bitcast.41, s32[2,512]{1,0:T(2,128)S(1)} %bitcast.30, f32[10,512]{1,0:T(8,128)S(1)} %copy-done, f32[10,512]{1,0:T(8,128)S(1)} %copy-done.2, f32[10,512]{1,0:T(8,128)S(1)} %copy-done.3, s32[1,128]{1,0:T(1,128)S(1)} %copy-done.9), custom_call_target="tpu_custom_call" | custom-call | tf_op jit(solution)/shard_map/pallas_call | solution.py:54
  5.6 0.1 reshape.44
  5.7 30.9 %all_to_all.38 = f32[128,2,128]{2,1,0:T(2,128)S(1)} all-to-all(f32[128,2,128]{2,1,0:T(2,128)S(1)} %reshape.44), channel_id=1, replica_groups=mesh['dev'=128,'rep'=4] {'dev'}, dimensions={0} | all-to-all | bytes 262144 | tf_op jit(solution)/shard_map/all_to_all | solution.py:437
  36.7 0.0 copy-start.1
  36.7 0.7 copy-done.1
  37.4 0.6 shard_map.112
  38.1 0.1 reshape.46
  38.1 17.8 %all_to_all.39 = f32[128,2,128]{2,1,0:T(2,128)S(1)} all-to-all(f32[128,2,128]{2,1,0:T(2,128)S(1)} %reshape.46), channel_id=1, replica_groups=mesh['dev'=128,'rep'=4] {'dev'}, dimensions={0} | all-to-all | bytes 262144 | tf_op jit(solution)/shard_map/all_to_all | solution.py:437
  55.9 0.0 copy-start.6
  55.9 0.0 copy-start.8
  55.9 0.0 copy-start.5
  55.9 0.0 copy-start.7
  55.9 0.7 copy-done.6
  56.6 0.0 copy-done.8
  56.6 0.0 copy-done.5
  56.6 0.0 copy-done.7
  56.6 7.3 %shard_map.113 = (f32[3,2,256]{2,1,0:T(2,128)}, f32[128,384]{1,0:T(8,128)S(1)}, f32[16,1024]{1,0:T(8,128)S(1)}) custom-call(f32[128,256]{1,0:T(8,128)S(1)} %bitcast.27, s32[1,1024]{1,0:T(1,128)S(1)} %bitcast.42, s32[2,512]{1,0:T(2,128)S(1)} %bitcast.31, s32[1,1024]{1,0:T(1,128)S(1)} %get-tuple-element.32.rank_ref, f32[3,2,256]{2,1,0:T(2,128)S(1)} %bitcast.32, ...), custom_call_target="tpu_custom_call" | custom-call | tf_op jit(solution)/shard_map/pallas_call | solution.py:54
  63.9 0.1 copy.15
  64.1 0.2 copy.16
  64.2 20.3 %all_to_all.40 = f32[128,3,128]{2,1,0:T(4,128)S(1)} all-to-all(f32[128,3,128]{2,1,0:T(4,128)S(1)} %copy.16), channel_id=1, replica_groups=mesh['dev'=128,'rep'=4] {'dev'}, dimensions={0} | all-to-all | bytes 393216 | tf_op jit(solution)/shard_map/all_to_all | solution.py:437
  84.5 0.1 copy.17
  84.6 0.1 copy.18.grad_ref
  84.8 1.4 %shard_map.114 = f32[16,512]{1,0:T(8,128)S(1)} custom-call(f32[128,384]{1,0:T(8,128)S(1)} %copy.18.grad_ref), custom_call_target="tpu_custom_call" | custom-call | tf_op jit(solution)/shard_map/pallas_call | solution.py:54
  86.2 0.7 broadcast_in_dim.6
  86.9 4.0 %all-to-all-start.6 = ((f32[4,16,512]{2,1,0:T(8,128)}), f32[4,16,512]{2,1,0:T(8,128)S(1)}, u32[]{:S(2)}, u32[]{:S(2)}) async-start(f32[4,16,512]{2,1,0:T(8,128)} %broadcast_in_dim.6), calls=%async_computation.6 | async-start | bytes 262144 | tf_op jit(solution)/shard_map/all_to_all | solution.py:442
  90.9 4.8 %all-to-all-done.6 = f32[4,16,512]{2,1,0:T(8,128)S(1)} async-done(((f32[4,16,512]{2,1,0:T(8,128)}), f32[4,16,512]{2,1,0:T(8,128)S(1)}, u32[]{:S(2)}, u32[]{:S(2)}) %all-to-all-start.6) | async-done | bytes 131104 | tf_op jit(solution)/shard_map/all_to_all | solution.py:442
  95.7 0.6 slice_reduce_fusion
  97.0 0.2 conditional.1
  97.2 0.9 shard_map.115
  (2 shorter events, 0.0 us)
Async XLA Ops:
  0.6 0.7 copy-start.9
  1.3 0.8 copy-start
  2.0 0.8 copy-start.2
  2.8 0.8 copy-start.3
  3.6 0.7 copy-start.4
  36.7 0.8 copy-start.1
  55.9 0.7 copy-start.6
  55.9 0.7 copy-start.8
  55.9 0.7 copy-start.5
  55.9 0.7 copy-start.7
  86.9 8.9 %all-to-all-start.6 = ((f32[4,16,512]{2,1,0:T(8,128)}), f32[4,16,512]{2,1,0:T(8,128)S(1)}, u32[]{:S(2)}, u32[]{:S(2)}) async-start(f32[4,16,512]{2,1,0:T(8,128)} %broadcast_in_dim.6), calls=%async_computation.6 | async-start | bytes 262144 | tf_op jit(solution)/shard_map/all_to_all | solution.py:442

commit v3 on v2

--- a/solution.py
+++ b/solution.py
@@ -11,10 +11,12 @@
 BACKGROUND = 0.5
 CAP = 16
 SUB = 4
-HOME_CAP = 32
-UNROLL = 4
+HOME_CAP = 25
+SENT = 10
+VALUES = 10
+UNROLL = 16
 ROWS = 16
-VMEM = 48 * 1024 * 1024
+VMEM = 40 * 1024 * 1024
 F32 = jnp.float32
 BF16 = jnp.bfloat16
 
@@ -44,23 +46,36 @@
     return lax.dot_general(a, b, (((1,), (1,)), ((), ())), preferred_element_type=F32)
 
 
-def call(body, out_shape, scratch=(), smem=()):
+def call(body, out_shape, scratch=(), smem=(), hbm=(), smem_out=(), hbm_out=(), vmem=VMEM):
     def run(*args):
-        specs = [
-            pl.BlockSpec(memory_space=pltpu.SMEM if i in smem else pltpu.VMEM)
+        space = [
+            pltpu.SMEM if i in smem else pl.ANY if i in hbm else pltpu.VMEM
             for i in range(len(args))
         ]
         outs = jax.tree.map(lambda _: pl.BlockSpec(memory_space=pltpu.VMEM), out_shape)
+        if smem_out or hbm_out:
+            outs = tuple(
+                pl.BlockSpec(
+                    memory_space=pltpu.SMEM if i in smem_out else pl.ANY if i in hbm_out else pltpu.VMEM
+                )
+                for i in range(len(out_shape))
+            )
         return pl.pallas_call(
             body,
             out_shape=out_shape,
-            in_specs=specs,
+            in_specs=[pl.BlockSpec(memory_space=m) for m in space],
             out_specs=outs,
             scratch_shapes=list(scratch),
-            compiler_params=pltpu.CompilerParams(vmem_limit_bytes=VMEM),
+            compiler_params=pltpu.CompilerParams(vmem_limit_bytes=vmem),
         )(*args)
 
     return run
+
+
+def start(source, place, sem):
+    copy = pltpu.make_async_copy(source, place, sem)
+    copy.start()
+    return copy
 
 
 def along(ref):
@@ -91,7 +106,7 @@
     return dot(homes, one_hot(iota((devices, gauss), 1) // sub == iota((devices, gauss), 0)))[0:1]
 
 
-def pack_blocks(stack, homes, devices):
+def pack_blocks(stack, homes, devices, rows):
     gauss = stack.shape[1]
     sub = gauss // devices
     place = iota((devices, gauss), 0) == homes.astype(jnp.int32)
@@ -99,70 +114,141 @@
     pick = jnp.concatenate([one_hot(place & (within == i)) for i in range(sub)], axis=0)
     moved = dot_t(jnp.concatenate(parts(stack), axis=0), pick)
     moved = moved[:32] + moved[32:64] + moved[64:]
-    return jnp.transpose(
-        jnp.concatenate([moved[:, i * devices : (i + 1) * devices] for i in range(sub)], axis=0)
-    )
-
-
-def place_blocks(came, gauss):
-    devices = came.shape[0]
-    sub = gauss // devices
-    came = jnp.transpose(came)
-    came = jnp.concatenate([came[i * 32 : (i + 1) * 32] for i in range(sub)], axis=1)
+    moved = [moved[:rows, i * devices : (i + 1) * devices] for i in range(sub)]
+    if sub * rows < 128:
+        moved.append(jnp.zeros((128 - sub * rows, devices), F32))
+    return jnp.transpose(jnp.concatenate(moved, axis=0))[:, : sub * rows]
+
+
+def place_blocks(blocks, devices):
+    sub = len(blocks)
+    gauss = sub * devices
     row = iota((gauss, gauss), 0)
     spot = one_hot(row % devices * sub + row // devices == iota((gauss, gauss), 1))
+    came = jnp.concatenate(blocks, axis=1)
     out = dot(jnp.concatenate(parts(came), axis=0), spot)
     return out[:32] + out[32:64] + out[64:]
 
 
+def sigmoid(x):
+    return 1.0 / (1.0 + jnp.exp(-x))
+
+
+def conics(rows):
+    conic_a, conic_c, skew = jnp.exp(rows[3:4]), jnp.exp(rows[5:6]), jnp.tanh(rows[4:5])
+    return conic_a, conic_c, skew, jnp.sqrt(conic_a * conic_c)
+
+
 def request_body(
-    owner_ref, index_ref, params_ref, moment1_ref, moment2_ref, rehome_ref,
-    request_ref, rank_ref, stack_s,
+    owner_hbm, index_hbm, moment2_hbm, rehome_hbm,
+    request_hbm, lists_hbm,
+    owner_s, index_s, moment2_s, rehome_s, stack_s, request_s, lists_s, sems,
 ):
-    gauss = params_ref.shape[1]
-    devices = request_ref.shape[0]
-    rank, named = rank_of(owner_ref[...], devices)
-    rank_ref[...] = rank
-    ids = along(index_ref)
+    copies = [
+        start(source, place, sems.at[n])
+        for n, (source, place) in enumerate(
+            [
+                (owner_hbm, owner_s), (index_hbm, index_s),
+                (rehome_hbm, rehome_s), (moment2_hbm, moment2_s),
+            ]
+        )
+    ]
+    gauss = moment2_s.shape[1]
+    devices = request_s.shape[0]
+    stack_s[...] = jnp.zeros_like(stack_s)
+    lists_s[...] = jnp.zeros_like(lists_s)
+    for copy in copies:
+        copy.wait()
+    owner, ids = owner_s[...], along(index_s)
+    rank, named = rank_of(owner, devices)
+    homes = homes_of(rehome_s, gauss)
+    lists_s[3:4, 0:gauss] = homes.astype(jnp.int32)
+    lists_s[0:1] = owner
+    lists_s[1:2] = ids
+    lists_s[2:3] = rank
+    kept = start(lists_s, lists_hbm, sems.at[4])
     slot = iota((CAP, ids.shape[1]), 0) == rank
     high = jnp.where(slot, (ids >> 4).astype(F32), 0.0)
     low = jnp.where(slot, (ids & 15).astype(F32), 0.0)
     total = dot_t(named, jnp.concatenate([high, low], axis=0).astype(BF16))
-    ids = 16.0 * total[:, :CAP] + total[:, CAP:]
+    asked = 16.0 * total[:, :CAP] + total[:, CAP:]
+    stack_s[0:10] = moment2_s[...]
+    blocks = pack_blocks(stack_s[...], homes, devices, 16)
+    zero = jnp.zeros((devices, 128 - CAP - blocks.shape[1]), F32)
+    request_s[...] = jnp.concatenate([blocks, asked, zero], axis=1)
+    sent = start(request_s, request_hbm, sems.at[5])
+    kept.wait()
+    sent.wait()
+
+
+def table_body(
+    params_ref, moment1_ref, camera_ref, lists_ref, target_ref,
+    table_ref, blocks_ref, kept_lists_ref, kept_target_ref, stack_s,
+):
+    kept_lists_ref[...] = lists_ref[...]
+    kept_target_ref[...] = target_ref[...]
+    gauss = params_ref.shape[1]
+    devices = blocks_ref.shape[1]
+    cam = [camera_ref[0, i] for i in range(8)]
+    homes = lists_ref[3:4, 0:gauss].astype(F32)
+    params = params_ref[...]
     stack_s[...] = jnp.zeros_like(stack_s)
-    stack_s[0:10] = params_ref[...]
+    stack_s[0:10] = params
     stack_s[10:20] = moment1_ref[...]
-    stack_s[20:30] = moment2_ref[...]
-    request_ref[:, 0:128] = pack_blocks(stack_s[...], homes_of(rehome_ref, gauss), devices)
-    request_ref[:, 128:256] = jnp.concatenate([ids, jnp.zeros((devices, 128 - CAP), F32)], axis=1)
+    blocks = pack_blocks(stack_s[...], homes, devices, 24)
+    zero = jnp.zeros((devices, 128 - blocks.shape[1]), F32)
+    blocks = jnp.transpose(jnp.concatenate([blocks, zero], axis=1))
+    blocks_ref[...] = blocks[: blocks_ref.shape[0]]
+    x, y, z = params[0:1], params[1:2], params[2:3]
+    conic_a, conic_c, skew, root = conics(params)
+    table_ref[...] = jnp.zeros_like(table_ref)
+    table_ref[0:1] = cam[0] * x + cam[1] * y + cam[2] * z + cam[3]
+    table_ref[1:2] = cam[4] * x + cam[5] * y + cam[6] * z + cam[7]
+    table_ref[2:3] = conic_a
+    table_ref[3:4] = 0.9 * skew * root
+    table_ref[4:5] = conic_c
+    table_ref[5:9] = sigmoid(params[6:10])
+    table_ref[9:10] = homes
 
 
 def asked_hot(request_ref, gauss):
     devices = request_ref.shape[0]
-    ids = jnp.transpose(request_ref[:, 128:256]).astype(jnp.int32)
+    ids = jnp.transpose(request_ref[...])[64 : 64 + CAP].astype(jnp.int32)
     return jnp.concatenate(
         [one_hot(iota((gauss, devices), 0) == ids[j : j + 1]) for j in range(CAP)], axis=1
     )
 
 
-def respond_body(request_ref, params_ref, rehome_ref, response_ref, table):
-    gauss = params_ref.shape[1]
+def respond_body(request_ref, table_ref, blocks_ref, response_ref, out_s):
+    gauss = table_ref.shape[1]
     devices = request_ref.shape[0]
-    table[...] = jnp.zeros_like(table)
-    table[0:10] = params_ref[...]
-    table[10:11] = homes_of(rehome_ref, gauss)
-    got = dot(jnp.concatenate(parts(table[...]), axis=0), asked_hot(request_ref, gauss))
+    got = dot(jnp.concatenate(parts(table_ref[...]), axis=0), asked_hot(request_ref, gauss))
     got = got[:ROWS] + got[ROWS : 2 * ROWS] + got[2 * ROWS :]
-    for half in range(2):
-        block = jnp.concatenate(
-            [got[:, j * devices : (j + 1) * devices] for j in range(half * 8, half * 8 + 8)],
-            axis=0,
-        )
-        response_ref[:, half * 128 : half * 128 + 128] = jnp.transpose(block)
-
-
-def sigmoid(x):
-    return 1.0 / (1.0 + jnp.exp(-x))
+    for j in range(CAP):
+        out_s[pl.ds(j, VALUES, stride=CAP), :] = got[:VALUES, j * devices : (j + 1) * devices]
+    out_s[VALUES * CAP :] = blocks_ref[...]
+    response_ref[:, :128] = jnp.transpose(out_s[:128])
+    response_ref[:, 128:] = jnp.transpose(out_s[128:])
+
+
+def settle(request_ref, response_ref, old_ref):
+    devices = request_ref.shape[0]
+    sub = old_ref.shape[1] // devices
+    first = jnp.transpose(request_ref[...])
+    second = jnp.transpose(response_ref[:, 128:])[VALUES * CAP - 128 :]
+    blocks = [
+        jnp.concatenate(
+            [second[i * 24 : i * 24 + 24], jnp.zeros((8, devices), F32)], axis=0
+        )
+        for i in range(sub)
+    ]
+    old_ref[0:20] = place_blocks(blocks, devices)[0:20]
+    blocks = [
+        jnp.concatenate([first[i * 16 : i * 16 + 16], jnp.zeros((16, devices), F32)], axis=0)
+        for i in range(sub)
+    ]
+    old_ref[20:30] = place_blocks(blocks, devices)[0:10]
+    old_ref[30:32] = jnp.zeros((2, old_ref.shape[1]), F32)
 
 
 def stacked(pieces):
@@ -175,34 +261,29 @@
 
 
 def composite_body(
-    response_ref, owner_ref, index_ref, rank_ref, target_ref, camera_ref,
+    response_ref, lists_ref, target_ref,
     image_ref, grad_ref, entry_ref,
-    alpha_s, run_s, slope_s, split_s, entry_s,
+    alpha_s, run_s, slope_s, split_s, entry_s, sent_s,
 ):
     devices = response_ref.shape[0]
-    entries = owner_ref.shape[1]
+    entries = lists_ref.shape[1]
     _, tiles, pix = target_ref.shape
     depth = entries // tiles
-    cam = [camera_ref[0, i] for i in range(8)]
-    owner, rank = owner_ref[...], rank_ref[...]
+    owner, ids, rank = lists_ref[0:1], lists_ref[1:2], lists_ref[2:3]
     named = one_hot(iota((devices, entries), 0) == owner)
     got = jnp.concatenate(
         [jnp.transpose(response_ref[:, :128]), jnp.transpose(response_ref[:, 128:])], axis=0
-    )
+    )[: VALUES * CAP]
     spread = sum(dot(piece, named) for piece in parts(got))
-    values = jnp.zeros((ROWS, entries), F32)
-    for j in range(CAP):
-        values = values + jnp.where(rank == j, spread[j * ROWS : (j + 1) * ROWS], 0.0)
-    x, y, z = values[0:1], values[1:2], values[2:3]
-    screen_u = cam[0] * x + cam[1] * y + cam[2] * z + cam[3]
-    screen_v = cam[4] * x + cam[5] * y + cam[6] * z + cam[7]
-    conic_a, conic_c, skew = jnp.exp(values[3:4]), jnp.exp(values[5:6]), jnp.tanh(values[4:5])
-    root = jnp.sqrt(conic_a * conic_c)
-    conic_b = 0.9 * skew * root
-    level = sigmoid(values[0:16])
-    opacity = level[6:7]
+    mine = iota((CAP, entries), 0) == rank
+    values = [
+        jnp.sum(jnp.where(mine, spread[r * CAP : (r + 1) * CAP], 0.0), axis=0, keepdims=True)
+        for r in range(VALUES)
+    ]
+    screen_u, screen_v, conic_a, conic_b, conic_c, opacity = values[:6]
     entry_s[...] = jnp.zeros_like(entry_s)
-    entry_s[0:3] = level[7:10]
+    for c in range(3):
+        entry_s[c : c + 1] = values[6 + c]
     colors = entry_s[0:8]
     peak, half_a, half_c = 0.99 * opacity, -0.5 * conic_a, -0.5 * conic_c
     across = iota((SIDE, depth), 0).astype(F32) - 7.5
@@ -334,65 +415,81 @@
     s_0, s_u, s_v, s_uu, s_uv, s_vv = [
         jnp.concatenate([s[n] for s in sums], axis=1) for n in range(6)
     ]
-    g_u = conic_a * s_u + conic_b * s_v
-    g_v = conic_b * s_u + conic_c * s_v
-    half_b = -0.5 * s_uv * conic_b
-    for c in range(3):
-        entry_s[c : c + 1] = cam[c] * g_u + cam[4 + c] * g_v
-    entry_s[3:4] = half_b - 0.5 * s_uu * conic_a
-    entry_s[4:5] = -0.9 * s_uv * (1.0 - skew * skew) * root
-    entry_s[5:6] = half_b - 0.5 * s_vv * conic_c
-    entry_s[6:7] = s_0 * (1.0 - opacity)
-    tint = jnp.concatenate(color_grads, axis=1)[0:3]
-    entry_s[7:10] = tint * level[7:10] * (1.0 - level[7:10])
-    entry_ref[...] = entry_s[...]
-    home = (values[10:11] + 0.5).astype(jnp.int32)
-    spot = owner * SUB + along(index_ref) % SUB
-    entry_s[10:11] = spot.astype(F32)
+    entry_s[0:1] = conic_a * s_u + conic_b * s_v
+    entry_s[1:2] = conic_b * s_u + conic_c * s_v
+    entry_s[2:3] = -0.5 * s_uu
+    entry_s[3:4] = -s_uv
+    entry_s[4:5] = -0.5 * s_vv
+    entry_s[5:6] = s_0 / opacity
+    entry_s[6:9] = jnp.concatenate(color_grads, axis=1)[0:3]
+    entry_s[9:10] = (owner * SUB + ids % SUB).astype(F32)
+    grads = entry_s[...]
+    entry_ref[...] = grads
+    home = (values[9] + 0.5).astype(jnp.int32)
     order, moves = rank_of(home, devices)
-    slots = iota((HOME_CAP, entries), 0) == order
-    grads = entry_s[...]
+    slots = iota((32, entries), 0) == jnp.where(order < HOME_CAP, order, 99)
     sent = 0.0
     for piece in parts(grads, 2):
         piece = piece.astype(F32)
         rows = jnp.concatenate(
-            [jnp.where(slots, piece[r : r + 1], 0.0).astype(BF16) for r in range(11)], axis=0
+            [jnp.where(slots, piece[r : r + 1], 0.0).astype(BF16) for r in range(SENT)], axis=0
         )
         sent = sent + dot_t(rows, moves)
+    for r in range(SENT):
+        sent_s[r * HOME_CAP : (r + 1) * HOME_CAP] = sent[r * 32 : r * 32 + HOME_CAP]
     over = jnp.max(order, axis=1, keepdims=True) >= HOME_CAP
-    flag = jnp.where(over, 1.0, 0.0) + jnp.zeros((HOME_CAP, devices), F32)
-    sent = jnp.concatenate([sent, flag], axis=0)
-    for n in range(3):
-        grad_ref[:, n * 128 : (n + 1) * 128] = jnp.transpose(sent[n * 128 : (n + 1) * 128])
-
-
-def collect_body(grad_ref, out_ref, came_s):
-    gauss = out_ref.shape[1]
+    flag = jnp.where(over, 1.0, 0.0) + jnp.zeros((256 - SENT * HOME_CAP, devices), F32)
+    sent_s[SENT * HOME_CAP :] = flag
+    grad_ref[:, :128] = jnp.transpose(sent_s[:128])
+    grad_ref[:, 128:] = jnp.transpose(sent_s[128:])
+
+
+def pull_back(total, old, camera_ref, out_ref):
+    cam = [camera_ref[0, i] for i in range(8)]
+    g_u, g_v, g_a, g_b, g_c = [total[r : r + 1] for r in range(5)]
+    conic_a, conic_c, skew, root = conics(old)
+    half_b = g_b * (0.45 * skew * root)
+    level = sigmoid(old[6:10])
+    rows = [
+        (0, cam[0] * g_u + cam[4] * g_v),
+        (1, cam[1] * g_u + cam[5] * g_v),
+        (2, cam[2] * g_u + cam[6] * g_v),
+        (3, g_a * conic_a + half_b),
+        (4, g_b * 0.9 * (1.0 - skew * skew) * root),
+        (5, g_c * conic_c + half_b),
+        (6, total[5:9] * level * (1.0 - level)),
+    ]
+    for copy in range(out_ref.shape[0]):
+        for r, value in rows:
+            out_ref[copy, r : r + value.shape[0]] = value
+
+
+def collect_body(grad_ref, request_ref, response_ref, camera_ref, out_ref, old_ref, came_s):
+    settle(request_ref, response_ref, old_ref)
+    gauss = out_ref.shape[2]
     devices = grad_ref.shape[0]
-    for n in range(3):
-        came_s[n * 128 : (n + 1) * 128] = jnp.transpose(grad_ref[:, n * 128 : (n + 1) * 128])
-    spots = (came_s[10 * HOME_CAP : 11 * HOME_CAP] + 0.5).astype(jnp.int32)
-    total = jnp.zeros((2 * ROWS, gauss), F32)
+    came_s[:128] = jnp.transpose(grad_ref[:, :128])
+    came_s[128:] = jnp.transpose(grad_ref[:, 128:])
+    spots = (came_s[9 * HOME_CAP : 10 * HOME_CAP] + 0.5).astype(jnp.int32)
+    hot, came = [], []
     zero = jnp.zeros((6, devices), F32)
-    for start in range(0, HOME_CAP, 8):
-        hot, came = [], []
-        for j in range(start, start + 8):
-            hot.append(one_hot(iota((gauss, devices), 0) == spots[j : j + 1]))
-            came.append(
-                jnp.concatenate([came_s[pl.ds(j, 10, stride=HOME_CAP), :], zero], axis=0)
-            )
-        came = parts(jnp.concatenate(came, axis=1), 2)
-        total = total + dot_t(jnp.concatenate(came, axis=0), jnp.concatenate(hot, axis=1))
-    out_ref[...] = total[:ROWS] + total[ROWS:]
-    flags = came_s[11 * HOME_CAP : 12 * HOME_CAP]
+    for j in range(HOME_CAP):
+        hot.append(one_hot(iota((gauss, devices), 0) == spots[j : j + 1]))
+        came.append(jnp.concatenate([came_s[pl.ds(j, SENT, stride=HOME_CAP), :], zero], axis=0))
+    came = parts(jnp.concatenate(came, axis=1), 2)
+    total = dot_t(jnp.concatenate(came, axis=0), jnp.concatenate(hot, axis=1))
+    out_ref[...] = jnp.zeros_like(out_ref)
+    pull_back(total[:ROWS] + total[ROWS:], old_ref[...], camera_ref, out_ref)
+    flags = came_s[SENT * HOME_CAP :]
     flag = jnp.max(jnp.max(flags, axis=1, keepdims=True), axis=0, keepdims=True)
-    out_ref[10:11] = flag + jnp.zeros((1, gauss), F32)
-
-
-def to_owner_body(entry_ref, owner_ref, rank_ref, out_ref):
+    for copy in range(out_ref.shape[0]):
+        out_ref[copy, 10:11] = flag + jnp.zeros((1, gauss), F32)
+
+
+def to_owner_body(entry_ref, lists_ref, out_ref):
     devices = out_ref.shape[0]
-    rank = rank_ref[...]
-    named = one_hot(iota((devices, rank.shape[1]), 0) == owner_ref[...])
+    rank = lists_ref[2:3]
+    named = one_hot(iota((devices, rank.shape[1]), 0) == lists_ref[0:1])
     grads = entry_ref[...]
     slots = jnp.concatenate([jnp.where(rank == j, grads, 0.0) for j in range(CAP)], axis=0)
     sent = sum(dot_t(piece, named) for piece in parts(slots))
@@ -400,7 +497,7 @@
     out_ref[:, 128:] = jnp.transpose(sent[128:])
 
 
-def at_owner_body(grad_ref, request_ref, rehome_ref, out_ref, *, gauss):
+def at_owner_body(grad_ref, request_ref, lists_ref, out_ref, *, gauss):
     devices = grad_ref.shape[0]
     came = jnp.concatenate(
         [jnp.transpose(grad_ref[:, :128]), jnp.transpose(grad_ref[:, 128:])], axis=0
@@ -409,16 +506,22 @@
     total = dot_t(jnp.concatenate(parts(came), axis=0), asked_hot(request_ref, gauss))
     total = total[:ROWS] + total[ROWS : 2 * ROWS] + total[2 * ROWS :]
     stack = jnp.concatenate([total, jnp.zeros_like(total)], axis=0)
-    out_ref[...] = pack_blocks(stack, homes_of(rehome_ref, gauss), devices)
-
-
-def at_home_body(came_ref, out_ref):
-    out_ref[...] = place_blocks(came_ref[...], out_ref.shape[1])[:ROWS]
-
-
-def adam_body(grads_ref, request_ref, params_ref, moment1_ref, moment2_ref):
-    old = place_blocks(request_ref[:, 0:128], params_ref.shape[1])
+    out_ref[...] = pack_blocks(stack, lists_ref[3:4, 0:gauss].astype(F32), devices, 32)
+
+
+def at_home_body(came_ref, old_ref, camera_ref, out_ref):
+    out_ref[...] = jnp.zeros_like(out_ref)
+    devices = came_ref.shape[0]
+    came = jnp.transpose(came_ref[...])
+    sub = old_ref.shape[1] // devices
+    total = place_blocks([came[i * 32 : (i + 1) * 32] for i in range(sub)], devices)
+    pull_back(total, old_ref[...], camera_ref, out_ref)
+
+
+def adam_body(grads_ref, old_ref, params_ref, moment1_ref, moment2_ref, full_ref):
+    old = old_ref[...]
     grad = (grads_ref[0] + grads_ref[1]) + (grads_ref[2] + grads_ref[3])
+    full_ref[0, 0] = (jnp.max(grad[10:11]) > 0.5).astype(jnp.int32)
     grad = grad[0:10]
     moment1 = 0.9 * old[10:20] + 0.1 * grad
     moment2 = 0.99 * old[20:30] + 0.01 * grad * grad
@@ -437,55 +540,82 @@
     return lax.all_to_all(parcel, "dev", 0, 0, tiled=True).reshape(x.shape)
 
 
-def share(x):
-    copies = jnp.broadcast_to(x[None], (lax.axis_size("rep"), *x.shape))
+def share(copies):
     return lax.all_to_all(copies, "rep", 0, 0, tiled=True)
 
 
 def local(params, moment1, moment2, camera, owner, local_index, target, rehome):
     devices = lax.axis_size("dev")
+    reps = lax.axis_size("rep")
     gauss = params.shape[1]
     _, tiles, depth = local_index.shape
     entries = tiles * depth
     pix = target.shape[3]
     owners = owner.reshape(1, entries)
     ids = local_index[0]
-    request, rank = call(
+    stack = pltpu.VMEM((32, gauss), F32)
+    request, lists = call(
         request_body,
-        (shape(devices, 256), shape(1, entries, dtype=jnp.int32)),
-        [pltpu.VMEM((32, gauss), F32)],
-    )(owners, ids, params, moment1, moment2, rehome)
+        (shape(devices, 128), shape(8, entries, dtype=jnp.int32)),
+        [
+            pltpu.VMEM((1, entries), jnp.int32), pltpu.VMEM((tiles, depth), jnp.int32),
+            pltpu.VMEM((10, gauss), F32), pltpu.VMEM((1, devices), jnp.int32), stack,
+            pltpu.VMEM((devices, 128), F32), pltpu.VMEM((8, entries), jnp.int32),
+            pltpu.SemaphoreType.DMA((6,)),
+        ],
+        hbm=(0, 1, 2, 3),
+        hbm_out=(0, 1),
+        vmem=60 * 1024 * 1024,
+    )(owners, ids, moment2, rehome)
     request = exchange(request)
-    response = call(respond_body, shape(devices, 256), [pltpu.VMEM((ROWS, gauss), F32)])(
-        request, params, rehome
+    table, blocks, lists, goal = call(
+        table_body,
+        (
+            shape(ROWS, gauss), shape(256 - VALUES * CAP, devices),
+            shape(8, entries, dtype=jnp.int32), shape(3, tiles, pix),
+        ),
+        [stack],
+        smem=(2,),
+    )(params, moment1, camera, lists, target[0].transpose(1, 0, 2))
+    response = call(respond_body, shape(devices, 256), [pltpu.VMEM((256, devices), F32)])(
+        request, table, blocks
     )
     response = exchange(response)
     plane = pltpu.VMEM((tiles * pix, depth), F32)
     images, grads, by_entry = call(
         composite_body,
-        (shape(3, tiles, pix), shape(devices, 384), shape(ROWS, entries)),
+        (shape(3, tiles, pix), shape(devices, 256), shape(ROWS, entries)),
         [
             plane, plane, plane, pltpu.VMEM((2, tiles * pix, depth), BF16),
-            pltpu.VMEM((ROWS, entries), F32),
+            pltpu.VMEM((ROWS, entries), F32), pltpu.VMEM((256, devices), F32),
         ],
-        smem=(5,),
-    )(response, owners, ids, rank, target[0].transpose(1, 0, 2), camera)
+    )(response, lists, goal)
     grads = exchange(grads)
-    grads = call(collect_body, shape(ROWS, gauss), [pltpu.VMEM((384, devices), F32)])(grads)
-    grads = share(grads)
-
-    def by_owner(grads, by_entry, owners, rank, request, rehome):
-        sent = call(to_owner_body, shape(devices, 256))(by_entry, owners, rank)
+    grads, old = call(
+        collect_body,
+        (shape(reps, ROWS, gauss), shape(32, gauss)),
+        [pltpu.VMEM((256, devices), F32)],
+        smem=(3,),
+    )(grads, request, response, camera)
+    update = call(
+        adam_body, (shape(10, gauss),) * 3 + (shape(1, 1, dtype=jnp.int32),), smem_out=(3,)
+    )
+    *out, full = update(share(grads), old)
+
+    def by_owner(out, by_entry, lists, request, old, camera):
+        sent = call(to_owner_body, shape(devices, 256))(by_entry, lists)
         sent = call(functools.partial(at_owner_body, gauss=gauss), shape(devices, 128))(
-            exchange(sent), request, rehome
-        )
-        return share(call(at_home_body, shape(ROWS, gauss))(exchange(sent)))
-
-    full = jnp.max(grads[:, 10, 0]) > 0.5
-    grads = lax.cond(
-        full, by_owner, lambda grads, *rest: grads, grads, by_entry, owners, rank, request, rehome
+            exchange(sent), request, lists
+        )
+        sent = call(at_home_body, shape(reps, ROWS, gauss), smem=(2,))(
+            exchange(sent), old, camera
+        )
+        return list(update(share(sent), old)[:3])
+
+    out = lax.cond(
+        full[0, 0] > 0, by_owner, lambda out, *rest: out,
+        list(out), by_entry, lists, request, old, camera,
     )
-    out = call(adam_body, (shape(10, gauss),) * 3)(grads, request)
     return (*out, images.transpose(1, 0, 2)[None])
 
 

time: 98.9 us -> 87.4 us (0.88)
  blocking collectives: 69 us -> 35.7 us
  starting transfers between devices: 4.03 us -> 22.6 us
  waiting for transfers between devices: 4.83 us -> 14.6 us
  local copies, waits for them, and re-layouts: 6.42 us -> 0.79 us
    all_to_all x3 -> x2, blocking collectives: 69 us -> 35.7 us  [exchange(): return lax.all_to_all(parcel, 'dev', 0, 0, tiled=True).reshape(x.shape)]
    all_to_all x0 -> x1, starting transfers between devices: none -> 18.6 us  [exchange(): return lax.all_to_all(parcel, 'dev', 0, 0, tiled=True).reshape(x.shape)]
    all_to_all x0 -> x1, waiting for transfers between devices: none -> 9.79 us  [exchange(): return lax.all_to_all(parcel, 'dev', 0, 0, tiled=True).reshape(x.shape)]
    unnamed x22 -> x12, local copies, waits for them, and re-layouts: 5.06 us -> 0.65 us
    pallas_call x5 -> x6, Pallas kernels: 11.7 us -> 11.5 us  [run(): pl.pallas_call(body, out_shape=out_shape, in_specs=[pl.BlockSpec(memory_s...]
  transfers between devices with their start and end apart: 1 -> 2, of which waited for: 1 -> 2; matrix products, arithmetic and copies ran while one was open for 0% -> 0% of each run, Pallas kernels for 0% -> 1%
where the time goes in v3:
time: 87.4 us; the launch traced here: 86.9 us
  blocking collectives  35.7 us (41%)
  starting transfers between devices  22.6 us (26%)
  waiting for transfers between devices  14.6 us (17%)
  Pallas kernels  11.5 us (13%)
  between operations  1.5 us (2%)
    all_to_all x2, blocking collectives, exchange(): return lax.all_to_all(parcel, 'dev', 0, 0, tiled=True).reshape(x.shape)  35.7 us
    all_to_all x1, starting transfers between devices, exchange(): return lax.all_to_all(parcel, 'dev', 0, 0, tiled=True).reshape(x.shape)  18.6 us
    pallas_call x6, Pallas kernels, run(): pl.pallas_call(body, out_shape=out_shape, in_specs=[pl.BlockSpec(memory_s...  11.5 us
    all_to_all x1, waiting for transfers between devices, exchange(): return lax.all_to_all(parcel, 'dev', 0, 0, tiled=True).reshape(x.shape)  9.79 us
    all_to_all x1, waiting for transfers between devices, share(): return lax.all_to_all(copies, 'rep', 0, 0, tiled=True)  4.83 us
    all_to_all x1, starting transfers between devices, share(): return lax.all_to_all(copies, 'rep', 0, 0, tiled=True)  4.02 us
  transfers between devices with their start and end apart: 2, of which 2 were waited for; matrix products, arithmetic and copies ran while one was open for 0% of the time, Pallas kernels for 1%

profile of v3, /device:TPU:1, one launch (start us, length us, event | category | flops | bytes accessed | tf_op | source)
XLA Modules:
  0.0 86.9 jit_solution(2197427960008497161)
XLA Ops:
  0.6 2.2 %shard_map.111 = (f32[128,128]{1,0:T(8,128)}, s32[8,1024]{1,0:T(8,128)}) custom-call(s32[1,1024]{1,0:T(1,128)} %bitcast.43, s32[2,512]{1,0:T(2,128)} %bitcast.44, f32[10,512]{1,0:T(8,128)} %moment2_hbm.1, s32[1,128]{1,0:T(1,128)} %rehome_hbm.1), custom_call_target="tpu_custom_call" | custom-call | tf_op jit(solution)/shard_map/pallas_call | solution.py:63
  2.9 0.0 copy-start
  2.9 0.0 copy-start.1
  2.9 0.0 copy-start.2
  2.9 0.0 copy-start.3
  2.9 18.6 %all-to-all-start.3 = ((f32[128,1,128]{2,1,0:T(1,128)}), f32[128,1,128]{2,1,0:T(1,128)S(1)}, u32[]{:S(2)}, u32[]{:S(2)}) async-start(f32[128,1,128]{2,1,0:T(1,128)} %bitcast.42), calls=%async_computation.3 | async-start | bytes 131072 | tf_op jit(solution)/shard_map/all_to_all | solution.py:540
  21.5 0.0 copy-start.4
  21.5 0.0 copy-done
  21.5 0.0 copy-done.1
  21.5 0.0 copy-done.2
  21.5 0.0 copy-done.3
  21.5 0.6 copy-done.4
  22.2 1.0 %shard_map.112 = (f32[16,512]{1,0:T(8,128)S(1)}, f32[96,128]{1,0:T(8,128)S(1)}, s32[8,1024]{1,0:T(8,128)S(1)}, f32[3,2,256]{2,1,0:T(2,128)S(1)}) custom-call(f32[10,512]{1,0:T(8,128)S(1)} %copy-done, f32[10,512]{1,0:T(8,128)S(1)} %copy-done.1, f32[1,8]{1,0:T(1,128)S(1)} %copy-done.4, s32[8,1024]{1,0:T(8,128)S(1)} %copy-done.2, f32[3,2,256]{2,1,0:T(2,128)S(1)} %bitcast.35), custom_call_target="tpu_custom_call" | custom-call | tf_op jit(solution)/shard_map/pallas_call | solution.py:63
  23.1 9.8 %all-to-all-done.3 = f32[128,1,128]{2,1,0:T(1,128)S(1)} async-done(((f32[128,1,128]{2,1,0:T(1,128)}), f32[128,1,128]{2,1,0:T(1,128)S(1)}, u32[]{:S(2)}, u32[]{:S(2)}) %all-to-all-start.3) | async-done | bytes 65568 | tf_op jit(solution)/shard_map/all_to_all | solution.py:540
  32.9 0.6 shard_map.113
  33.6 0.1 reshape.48
  33.7 17.9 %all_to_all.35 = f32[128,2,128]{2,1,0:T(2,128)S(1)} all-to-all(f32[128,2,128]{2,1,0:T(2,128)S(1)} %reshape.48), channel_id=1, replica_groups=mesh['dev'=128,'rep'=4] {'dev'}, dimensions={0} | all-to-all | bytes 262144 | tf_op jit(solution)/shard_map/all_to_all | solution.py:540
  51.6 4.4 %shard_map.114 = (f32[3,2,256]{2,1,0:T(2,128)}, f32[128,256]{1,0:T(8,128)S(1)}, f32[16,1024]{1,0:T(8,128)S(1)}) custom-call(f32[128,256]{1,0:T(8,128)S(1)} %bitcast.29, s32[8,1024]{1,0:T(8,128)S(1)} %get-tuple-element.50.lists_ref, f32[3,2,256]{2,1,0:T(2,128)S(1)} %get-tuple-element.51.target_ref), custom_call_target="tpu_custom_call" | custom-call | tf_op jit(solution)/shard_map/pallas_call | solution.py:63
  56.0 0.1 reshape.50
  56.0 17.8 %all_to_all.36 = f32[128,2,128]{2,1,0:T(2,128)S(1)} all-to-all(f32[128,2,128]{2,1,0:T(2,128)S(1)} %reshape.50), channel_id=1, replica_groups=mesh['dev'=128,'rep'=4] {'dev'}, dimensions={0} | all-to-all | bytes 262144 | tf_op jit(solution)/shard_map/all_to_all | solution.py:540
  73.8 2.6 %shard_map.115 = (f32[4,16,512]{2,1,0:T(8,128)}, f32[32,512]{1,0:T(8,128)S(1)}) custom-call(f32[128,256]{1,0:T(8,128)S(1)} %bitcast.31, f32[128,128]{1,0:T(8,128)S(1)} %bitcast.37, f32[128,256]{1,0:T(8,128)S(1)} %bitcast.30, f32[1,8]{1,0:T(1,128)S(1)} %copy-done.4), custom_call_target="tpu_custom_call" | custom-call | tf_op jit(solution)/shard_map/pallas_call | solution.py:63
  76.4 4.0 %all-to-all-start.6 = ((f32[4,16,512]{2,1,0:T(8,128)}), f32[4,16,512]{2,1,0:T(8,128)S(1)}, u32[]{:S(2)}, u32[]{:S(2)}) async-start(f32[4,16,512]{2,1,0:T(8,128)} %get-tuple-element.53), calls=%async_computation.6 | async-start | bytes 262144 | tf_op jit(solution)/shard_map/all_to_all | solution.py:544
  80.4 4.8 %all-to-all-done.6.grads_ref = f32[4,16,512]{2,1,0:T(8,128)S(1)} async-done(((f32[4,16,512]{2,1,0:T(8,128)}), f32[4,16,512]{2,1,0:T(8,128)S(1)}, u32[]{:S(2)}, u32[]{:S(2)}) %all-to-all-start.6) | async-done | bytes 131104 | tf_op jit(solution)/shard_map/all_to_all | solution.py:544
  85.3 0.7 shard_map.116
  86.5 0.2 conditional.1
  (2 shorter events, 0.0 us)
Async XLA Ops:
  2.9 18.6 %copy-start = (f32[10,512]{1,0:T(8,128)S(1)}, f32[10,512]{1,0:T(8,128)}, u32[]{:S(2)}) copy-start(f32[10,512]{1,0:T(8,128)} %params_ref.1) | copy-start | bytes 61444
  2.9 18.6 %copy-start.1 = (f32[10,512]{1,0:T(8,128)S(1)}, f32[10,512]{1,0:T(8,128)}, u32[]{:S(2)}) copy-start(f32[10,512]{1,0:T(8,128)} %moment1_ref.1) | copy-start | bytes 61444
  2.9 18.6 %copy-start.2 = (s32[8,1024]{1,0:T(8,128)S(1)}, s32[8,1024]{1,0:T(8,128)}, u32[]{:S(2)}) copy-start(s32[8,1024]{1,0:T(8,128)} %get-tuple-element.47.lists_ref) | copy-start | bytes 98308
  2.9 18.6 %copy-start.3 = (f32[1,2,3,256]{3,1,2,0:T(2,128)S(1)}, f32[1,2,3,256]{3,1,2,0:T(2,128)}, u32[]{:S(2)}) copy-start(f32[1,2,3,256]{3,1,2,0:T(2,128)} %param.16) | copy-start | bytes 18436
  2.9 30.0 %all-to-all-start.3 = ((f32[128,1,128]{2,1,0:T(1,128)}), f32[128,1,128]{2,1,0:T(1,128)S(1)}, u32[]{:S(2)}, u32[]{:S(2)}) async-start(f32[128,1,128]{2,1,0:T(1,128)} %bitcast.42), calls=%async_computation.3 | async-start | bytes 131072 | tf_op jit(solution)/shard_map/all_to_all | solution.py:540
  21.5 0.7 copy-start.4
  76.4 8.8 %all-to-all-start.6 = ((f32[4,16,512]{2,1,0:T(8,128)}), f32[4,16,512]{2,1,0:T(8,128)S(1)}, u32[]{:S(2)}, u32[]{:S(2)}) async-start(f32[4,16,512]{2,1,0:T(8,128)} %get-tuple-element.53), calls=%async_computation.6 | async-start | bytes 262144 | tf_op jit(solution)/shard_map/all_to_all | solution.py:544

commit v4 on v3

--- a/solution.py
+++ b/solution.py
@@ -86,17 +86,16 @@
     entries = device.shape[1]
     step = 256
     before = one_hot(iota((step, step), 0) < iota((step, step), 1))
+    steps = [device[:, start : start + step] for start in range(0, entries, step)]
+    named = [jnp.where(iota((devices, step), 0) == d, 1.0, 0.0) for d in steps]
+    count = dot(jnp.concatenate(named, axis=0).astype(BF16), before)
     base = jnp.zeros((devices, 1), F32)
-    ranks, hots = [], []
-    for start in range(0, entries, step):
-        named = jnp.where(
-            iota((devices, step), 0) == device[:, start : start + step], 1.0, 0.0
-        )
-        hots.append(named.astype(BF16))
-        count = dot(hots[-1], before) + base
-        base = base + jnp.sum(named, axis=1, keepdims=True)
-        ranks.append(jnp.sum(named * count, axis=0, keepdims=True).astype(jnp.int32))
-    return jnp.concatenate(ranks, axis=1), jnp.concatenate(hots, axis=1)
+    ranks = []
+    for n, hot in enumerate(named):
+        place = count[n * devices : (n + 1) * devices] + base
+        base = base + jnp.sum(hot, axis=1, keepdims=True)
+        ranks.append(jnp.sum(hot * place, axis=0, keepdims=True).astype(jnp.int32))
+    return jnp.concatenate(ranks, axis=1), jnp.concatenate(named, axis=1).astype(BF16)
 
 
 def homes_of(rehome_ref, gauss):
@@ -120,14 +119,10 @@
     return jnp.transpose(jnp.concatenate(moved, axis=0))[:, : sub * rows]
 
 
-def place_blocks(blocks, devices):
-    sub = len(blocks)
-    gauss = sub * devices
+def in_order(gauss, devices):
+    sub = gauss // devices
     row = iota((gauss, gauss), 0)
-    spot = one_hot(row % devices * sub + row // devices == iota((gauss, gauss), 1))
-    came = jnp.concatenate(blocks, axis=1)
-    out = dot(jnp.concatenate(parts(came), axis=0), spot)
-    return out[:32] + out[32:64] + out[64:]
+    return one_hot(row % devices * sub + row // devices == iota((gauss, gauss), 1))
 
 
 def sigmoid(x):
@@ -183,7 +178,7 @@
 
 def table_body(
     params_ref, moment1_ref, camera_ref, lists_ref, target_ref,
-    table_ref, blocks_ref, kept_lists_ref, kept_target_ref, stack_s,
+    table_ref, blocks_ref, kept_lists_ref, kept_target_ref, order_ref, stack_s,
 ):
     kept_lists_ref[...] = lists_ref[...]
     kept_target_ref[...] = target_ref[...]
@@ -191,6 +186,7 @@
     devices = blocks_ref.shape[1]
     cam = [camera_ref[0, i] for i in range(8)]
     homes = lists_ref[3:4, 0:gauss].astype(F32)
+    order_ref[...] = in_order(gauss, devices)
     params = params_ref[...]
     stack_s[...] = jnp.zeros_like(stack_s)
     stack_s[0:10] = params
@@ -220,10 +216,21 @@
 
 
 def respond_body(request_ref, table_ref, blocks_ref, response_ref, out_s):
-    gauss = table_ref.shape[1]
     devices = request_ref.shape[0]
-    got = dot(jnp.concatenate(parts(table_ref[...]), axis=0), asked_hot(request_ref, gauss))
-    got = got[:ROWS] + got[ROWS : 2 * ROWS] + got[2 * ROWS :]
+    sub = table_ref.shape[1] // devices
+    ids = jnp.transpose(request_ref[...])[64 : 64 + CAP].astype(jnp.int32)
+    ids = jnp.concatenate([ids[j : j + 1] for j in range(CAP)], axis=1)
+    hot = one_hot(iota((devices, ids.shape[1]), 0) == ids % devices)
+    pieces = parts(table_ref[...])
+    tables = [
+        piece[:, i * devices : (i + 1) * devices] for piece in pieces for i in range(sub)
+    ]
+    all_got = dot(jnp.concatenate(tables, axis=0), hot)
+    span = sub * ROWS
+    all_got = all_got[:span] + all_got[span : 2 * span] + all_got[2 * span :]
+    got = jnp.zeros((ROWS, ids.shape[1]), F32)
+    for i in range(sub):
+        got = got + jnp.where(ids // devices == i, all_got[i * ROWS : (i + 1) * ROWS], 0.0)
     for j in range(CAP):
         out_s[pl.ds(j, VALUES, stride=CAP), :] = got[:VALUES, j * devices : (j + 1) * devices]
     out_s[VALUES * CAP :] = blocks_ref[...]
@@ -236,19 +243,10 @@
     sub = old_ref.shape[1] // devices
     first = jnp.transpose(request_ref[...])
     second = jnp.transpose(response_ref[:, 128:])[VALUES * CAP - 128 :]
-    blocks = [
-        jnp.concatenate(
-            [second[i * 24 : i * 24 + 24], jnp.zeros((8, devices), F32)], axis=0
-        )
-        for i in range(sub)
-    ]
-    old_ref[0:20] = place_blocks(blocks, devices)[0:20]
-    blocks = [
-        jnp.concatenate([first[i * 16 : i * 16 + 16], jnp.zeros((16, devices), F32)], axis=0)
-        for i in range(sub)
-    ]
-    old_ref[20:30] = place_blocks(blocks, devices)[0:10]
-    old_ref[30:32] = jnp.zeros((2, old_ref.shape[1]), F32)
+    for i in range(sub):
+        cols = slice(i * devices, (i + 1) * devices)
+        old_ref[0:24, cols] = second[i * 24 : i * 24 + 24]
+        old_ref[24:40, cols] = first[i * 16 : i * 16 + 16]
 
 
 def stacked(pieces):
@@ -263,7 +261,7 @@
 def composite_body(
     response_ref, lists_ref, target_ref,
     image_ref, grad_ref, entry_ref,
-    alpha_s, run_s, slope_s, split_s, entry_s, sent_s,
+    alpha_s, run_s, slope_s, split_s, entry_s,
 ):
     devices = response_ref.shape[0]
     entries = lists_ref.shape[1]
@@ -274,7 +272,9 @@
     got = jnp.concatenate(
         [jnp.transpose(response_ref[:, :128]), jnp.transpose(response_ref[:, 128:])], axis=0
     )[: VALUES * CAP]
-    spread = sum(dot(piece, named) for piece in parts(got))
+    spread = dot(jnp.concatenate(parts(got), axis=0), named)
+    span = VALUES * CAP
+    spread = spread[:span] + spread[span : 2 * span] + spread[2 * span :]
     mine = iota((CAP, entries), 0) == rank
     values = [
         jnp.sum(jnp.where(mine, spread[r * CAP : (r + 1) * CAP], 0.0), axis=0, keepdims=True)
@@ -283,7 +283,7 @@
     screen_u, screen_v, conic_a, conic_b, conic_c, opacity = values[:6]
     entry_s[...] = jnp.zeros_like(entry_s)
     for c in range(3):
-        entry_s[c : c + 1] = values[6 + c]
+        entry_s[c : c + 1] = values[6 + c] - BACKGROUND
     colors = entry_s[0:8]
     peak, half_a, half_c = 0.99 * opacity, -0.5 * conic_a, -0.5 * conic_c
     across = iota((SIDE, depth), 0).astype(F32) - 7.5
@@ -324,9 +324,6 @@
         dot(split_s[0, :, half:], tri) + dot(split_s[1, :, half:], tri)
         + dot(split_s[0, :, :half], full) + dot(split_s[1, :, :half], full)
     )
-    ones = jnp.ones((16, depth), BF16)
-    behind = dot_t(ones, split_s[0]) + dot_t(ones, split_s[1])
-    behind = BACKGROUND * jnp.exp(behind[0:1])
     for t in range(tiles):
 
         def weigh(t, i, carry):
@@ -337,27 +334,24 @@
             return carry
 
         over_rows(weigh, 0, t)
-    color_grads, tails = [], []
+    color_grads = []
     for t in range(tiles):
         px = slice(t * pix, (t + 1) * pix)
         paints = parts(colors[:, of(t)])
         paint = stacked(paints)
         shown = groups(dot_t(paint, split_s[0, px]) + dot_t(paint, split_s[1, px]))
-        shown = shown + behind[:, px]
+        shown = shown + BACKGROUND
         gaps = []
         for c in range(3):
             image_ref[c, t : t + 1] = shown[c : c + 1]
             gaps.append(shown[c : c + 1] - target_ref[c, t : t + 1])
-        tail = behind[:, px] * (gaps[0] + gaps[1] + gaps[2])
         gap = jnp.concatenate([*gaps, jnp.zeros((5, pix), F32)], axis=0)
         gap_parts = parts(gap)
         drawn = stacked(gap_parts)
         color_grads.append(groups(dot(drawn, split_s[0, px]) + dot(drawn, split_s[1, px])))
         high, middle, low = [piece.astype(F32) for piece in gap_parts]
-        ends = [piece.astype(F32) for piece in parts(tail)]
-        ends = jnp.concatenate([*ends, jnp.zeros((5, pix), F32)], axis=0)
         left = jnp.concatenate(
-            [high, high, high, middle, middle, low, ends, jnp.zeros((72, pix), F32)], axis=0
+            [high, high, high, middle, middle, low, jnp.zeros((80, pix), F32)], axis=0
         )
         left = jnp.concatenate(
             [jnp.transpose(left[:, :128]), jnp.transpose(left[:, 128:])], axis=0
@@ -367,8 +361,6 @@
             [high, middle, low, high, middle, high, jnp.zeros((80, depth), F32)], axis=0
         ).astype(BF16)
         slope_s[px] = dot(left, right)
-        row = iota((128, depth), 0)
-        tails.append(dot(left, one_hot((row >= 48) & (row < 51))))
     for t in range(tiles):
 
         def spread_back(t, i, carry):
@@ -380,17 +372,11 @@
 
         over_rows(spread_back, 0, t)
     tri = one_hot(iota((half, half), 0) > iota((half, half), 1))
-    for t in range(tiles):
-        px = slice(t * pix, (t + 1) * pix)
-        run_s[px, half:] = (
-            dot(split_s[0, px, half:], tri) + dot(split_s[1, px, half:], tri)
-            + tails[t][:, half:]
-        )
-        run_s[px, :half] = (
-            dot(split_s[0, px, :half], tri) + dot(split_s[1, px, :half], tri)
-            + dot(split_s[0, px, half:], full) + dot(split_s[1, px, half:], full)
-            + tails[t][:, :half]
-        )
+    run_s[:, half:] = dot(split_s[0, :, half:], tri) + dot(split_s[1, :, half:], tri)
+    run_s[:, :half] = (
+        dot(split_s[0, :, :half], tri) + dot(split_s[1, :, :half], tri)
+        + dot(split_s[0, :, half:], full) + dot(split_s[1, :, half:], full)
+    )
     sums = []
     for t in range(tiles):
 
@@ -427,21 +413,28 @@
     entry_ref[...] = grads
     home = (values[9] + 0.5).astype(jnp.int32)
     order, moves = rank_of(home, devices)
-    slots = iota((32, entries), 0) == jnp.where(order < HOME_CAP, order, 99)
-    sent = 0.0
-    for piece in parts(grads, 2):
-        piece = piece.astype(F32)
-        rows = jnp.concatenate(
-            [jnp.where(slots, piece[r : r + 1], 0.0).astype(BF16) for r in range(SENT)], axis=0
-        )
-        sent = sent + dot_t(rows, moves)
-    for r in range(SENT):
-        sent_s[r * HOME_CAP : (r + 1) * HOME_CAP] = sent[r * 32 : r * 32 + HOME_CAP]
+    lanes = grad_ref.shape[1]
+    row = iota((8, entries), 0)
+    pieces = [piece.astype(F32) for piece in parts(grads, 2)]
+    sent = [[], []]
+    for start_row in range(0, lanes, 8):
+        c, last = start_row // HOME_CAP, (start_row + 7) // HOME_CAP
+        here = row == order - (start_row - c * HOME_CAP)
+        if last > c:
+            first = row < last * HOME_CAP - start_row
+            here = (here & first) | (row == order - (start_row - last * HOME_CAP))
+        for n in range(2):
+            value = pieces[n][c : c + 1]
+            if last > c:
+                value = jnp.where(first, value, pieces[n][last : last + 1])
+            sent[n].append(jnp.where(here, value, 0.0))
+    sent = [jnp.concatenate(rows, axis=0).astype(BF16) for rows in sent]
+    sent = dot_t(jnp.concatenate(sent, axis=0), moves)
+    sent = sent[:lanes] + sent[lanes:]
+    sent = jnp.concatenate([jnp.transpose(sent[:128]), jnp.transpose(sent[128:])], axis=1)
     over = jnp.max(order, axis=1, keepdims=True) >= HOME_CAP
-    flag = jnp.where(over, 1.0, 0.0) + jnp.zeros((256 - SENT * HOME_CAP, devices), F32)
-    sent_s[SENT * HOME_CAP :] = flag
-    grad_ref[:, :128] = jnp.transpose(sent_s[:128])
-    grad_ref[:, 128:] = jnp.transpose(sent_s[128:])
+    flag = jnp.where(over, 1.0, 0.0)
+    grad_ref[...] = jnp.where(iota((devices, lanes), 1) < SENT * HOME_CAP, sent, flag)
 
 
 def pull_back(total, old, camera_ref, out_ref):
@@ -450,40 +443,46 @@
     conic_a, conic_c, skew, root = conics(old)
     half_b = g_b * (0.45 * skew * root)
     level = sigmoid(old[6:10])
-    rows = [
-        (0, cam[0] * g_u + cam[4] * g_v),
-        (1, cam[1] * g_u + cam[5] * g_v),
-        (2, cam[2] * g_u + cam[6] * g_v),
-        (3, g_a * conic_a + half_b),
-        (4, g_b * 0.9 * (1.0 - skew * skew) * root),
-        (5, g_c * conic_c + half_b),
-        (6, total[5:9] * level * (1.0 - level)),
-    ]
-    for copy in range(out_ref.shape[0]):
-        for r, value in rows:
-            out_ref[copy, r : r + value.shape[0]] = value
-
-
-def collect_body(grad_ref, request_ref, response_ref, camera_ref, out_ref, old_ref, came_s):
+    out_ref[0:1] = cam[0] * g_u + cam[4] * g_v
+    out_ref[1:2] = cam[1] * g_u + cam[5] * g_v
+    out_ref[2:3] = cam[2] * g_u + cam[6] * g_v
+    out_ref[3:4] = g_a * conic_a + half_b
+    out_ref[4:5] = g_b * 0.9 * (1.0 - skew * skew) * root
+    out_ref[5:6] = g_c * conic_c + half_b
+    out_ref[6:10] = total[5:9] * level * (1.0 - level)
+
+
+def collect_body(
+    grad_ref, request_ref, response_ref, camera_ref, out_hbm, old_ref, came_s, total_s, sems
+):
     settle(request_ref, response_ref, old_ref)
-    gauss = out_ref.shape[2]
     devices = grad_ref.shape[0]
+    sub = old_ref.shape[1] // devices
     came_s[:128] = jnp.transpose(grad_ref[:, :128])
     came_s[128:] = jnp.transpose(grad_ref[:, 128:])
     spots = (came_s[9 * HOME_CAP : 10 * HOME_CAP] + 0.5).astype(jnp.int32)
+    blocks, places = spots // sub, spots % sub
     hot, came = [], []
     zero = jnp.zeros((6, devices), F32)
     for j in range(HOME_CAP):
-        hot.append(one_hot(iota((gauss, devices), 0) == spots[j : j + 1]))
-        came.append(jnp.concatenate([came_s[pl.ds(j, SENT, stride=HOME_CAP), :], zero], axis=0))
+        hot.append(one_hot(iota((devices, devices), 0) == blocks[j : j + 1]))
+        slot = jnp.concatenate([came_s[pl.ds(j, SENT, stride=HOME_CAP), :], zero], axis=0)
+        place = places[j : j + 1]
+        came.append(
+            jnp.concatenate([jnp.where(place == i, slot, 0.0) for i in range(sub)], axis=0)
+        )
     came = parts(jnp.concatenate(came, axis=1), 2)
     total = dot_t(jnp.concatenate(came, axis=0), jnp.concatenate(hot, axis=1))
-    out_ref[...] = jnp.zeros_like(out_ref)
-    pull_back(total[:ROWS] + total[ROWS:], old_ref[...], camera_ref, out_ref)
+    total = total[: sub * ROWS] + total[sub * ROWS :]
+    total = jnp.concatenate([total[i * ROWS : (i + 1) * ROWS] for i in range(sub)], axis=1)
+    total_s[...] = jnp.zeros_like(total_s)
+    pull_back(total, old_ref[...], camera_ref, total_s)
     flags = came_s[SENT * HOME_CAP :]
     flag = jnp.max(jnp.max(flags, axis=1, keepdims=True), axis=0, keepdims=True)
-    for copy in range(out_ref.shape[0]):
-        out_ref[copy, 10:11] = flag + jnp.zeros((1, gauss), F32)
+    total_s[10:11] = flag + jnp.zeros((1, total_s.shape[1]), F32)
+    copies = [start(total_s, out_hbm.at[n], sems.at[n]) for n in range(out_hbm.shape[0])]
+    for copy in copies:
+        copy.wait()
 
 
 def to_owner_body(entry_ref, lists_ref, out_ref):
@@ -509,25 +508,35 @@
     out_ref[...] = pack_blocks(stack, lists_ref[3:4, 0:gauss].astype(F32), devices, 32)
 
 
-def at_home_body(came_ref, old_ref, camera_ref, out_ref):
-    out_ref[...] = jnp.zeros_like(out_ref)
+def at_home_body(came_ref, old_ref, camera_ref, out_ref, total_s):
     devices = came_ref.shape[0]
     came = jnp.transpose(came_ref[...])
     sub = old_ref.shape[1] // devices
-    total = place_blocks([came[i * 32 : (i + 1) * 32] for i in range(sub)], devices)
-    pull_back(total, old_ref[...], camera_ref, out_ref)
-
-
-def adam_body(grads_ref, old_ref, params_ref, moment1_ref, moment2_ref, full_ref):
+    total = jnp.concatenate([came[i * 32 : i * 32 + ROWS] for i in range(sub)], axis=1)
+    total_s[...] = jnp.zeros_like(total_s)
+    pull_back(total, old_ref[...], camera_ref, total_s)
+    for copy in range(out_ref.shape[0]):
+        out_ref[copy] = total_s[...]
+
+
+def adam_body(
+    grads_ref, old_ref, order_ref, params_ref, moment1_ref, moment2_ref, full_ref, stack_s
+):
     old = old_ref[...]
     grad = (grads_ref[0] + grads_ref[1]) + (grads_ref[2] + grads_ref[3])
     full_ref[0, 0] = (jnp.max(grad[10:11]) > 0.5).astype(jnp.int32)
     grad = grad[0:10]
     moment1 = 0.9 * old[10:20] + 0.1 * grad
-    moment2 = 0.99 * old[20:30] + 0.01 * grad * grad
-    params_ref[...] = old[0:10] - 0.01 * moment1 / (jnp.sqrt(moment2) + 1e-08)
-    moment1_ref[...] = moment1
-    moment2_ref[...] = moment2
+    moment2 = 0.99 * old[24:34] + 0.01 * grad * grad
+    stack_s[...] = jnp.zeros_like(stack_s)
+    stack_s[0:10] = old[0:10] - 0.01 * moment1 / (jnp.sqrt(moment2) + 1e-08)
+    stack_s[16:26] = moment1
+    stack_s[32:42] = moment2
+    new = dot(jnp.concatenate(parts(stack_s[...]), axis=0), order_ref[...])
+    new = new[:48] + new[48:96] + new[96:]
+    params_ref[...] = new[0:10]
+    moment1_ref[...] = new[16:26]
+    moment2_ref[...] = new[32:42]
 
 
 def shape(*dims, dtype=F32):
@@ -568,11 +577,12 @@
         vmem=60 * 1024 * 1024,
     )(owners, ids, moment2, rehome)
     request = exchange(request)
-    table, blocks, lists, goal = call(
+    table, blocks, lists, goal, order = call(
         table_body,
         (
             shape(ROWS, gauss), shape(256 - VALUES * CAP, devices),
             shape(8, entries, dtype=jnp.int32), shape(3, tiles, pix),
+            shape(gauss, gauss, dtype=BF16),
         ),
         [stack],
         smem=(2,),
@@ -587,34 +597,41 @@
         (shape(3, tiles, pix), shape(devices, 256), shape(ROWS, entries)),
         [
             plane, plane, plane, pltpu.VMEM((2, tiles * pix, depth), BF16),
-            pltpu.VMEM((ROWS, entries), F32), pltpu.VMEM((256, devices), F32),
+            pltpu.VMEM((ROWS, entries), F32),
         ],
     )(response, lists, goal)
     grads = exchange(grads)
     grads, old = call(
         collect_body,
-        (shape(reps, ROWS, gauss), shape(32, gauss)),
-        [pltpu.VMEM((256, devices), F32)],
+        (shape(reps, ROWS, gauss), shape(40, gauss)),
+        [
+            pltpu.VMEM((256, devices), F32), pltpu.VMEM((ROWS, gauss), F32),
+            pltpu.SemaphoreType.DMA((reps,)),
+        ],
         smem=(3,),
+        hbm_out=(0,),
     )(grads, request, response, camera)
     update = call(
-        adam_body, (shape(10, gauss),) * 3 + (shape(1, 1, dtype=jnp.int32),), smem_out=(3,)
-    )
-    *out, full = update(share(grads), old)
-
-    def by_owner(out, by_entry, lists, request, old, camera):
+        adam_body,
+        (shape(10, gauss),) * 3 + (shape(1, 1, dtype=jnp.int32),),
+        [pltpu.VMEM((48, gauss), F32)],
+        smem_out=(3,),
+    )
+    *out, full = update(share(grads), old, order)
+
+    def by_owner(out, by_entry, lists, request, old, order, camera):
         sent = call(to_owner_body, shape(devices, 256))(by_entry, lists)
         sent = call(functools.partial(at_owner_body, gauss=gauss), shape(devices, 128))(
             exchange(sent), request, lists
         )
-        sent = call(at_home_body, shape(reps, ROWS, gauss), smem=(2,))(
-            exchange(sent), old, camera
-        )
-        return list(update(share(sent), old)[:3])
+        sent = call(
+            at_home_body, shape(reps, ROWS, gauss), [pltpu.VMEM((ROWS, gauss), F32)], smem=(2,)
+        )(exchange(sent), old, camera)
+        return list(update(share(sent), old, order)[:3])
 
     out = lax.cond(
         full[0, 0] > 0, by_owner, lambda out, *rest: out,
-        list(out), by_entry, lists, request, old, camera,
+        list(out), by_entry, lists, request, old, order, camera,
     )
     return (*out, images.transpose(1, 0, 2)[None])
 

time: 87.4 us -> 86.5 us (0.990)
  no operation moved by 1% of the time
where the time goes in v4:
time: 86.5 us; the launch traced here: 86.1 us
  blocking collectives  35.7 us (41%)
  starting transfers between devices  22.6 us (26%)
  waiting for transfers between devices  14.4 us (17%)
  Pallas kernels  10.9 us (13%)
  between operations  1.49 us (2%)
    all_to_all x2, blocking collectives, exchange(): return lax.all_to_all(parcel, 'dev', 0, 0, tiled=True).reshape(x.shape)  35.7 us
    all_to_all x1, starting transfers between devices, exchange(): return lax.all_to_all(parcel, 'dev', 0, 0, tiled=True).reshape(x.shape)  18.6 us
    pallas_call x6, Pallas kernels, run(): pl.pallas_call(body, out_shape=out_shape, in_specs=[pl.BlockSpec(memory_s...  10.9 us
    all_to_all x1, waiting for transfers between devices, exchange(): return lax.all_to_all(parcel, 'dev', 0, 0, tiled=True).reshape(x.shape)  9.6 us
    all_to_all x1, waiting for transfers between devices, share(): return lax.all_to_all(copies, 'rep', 0, 0, tiled=True)  4.83 us
    all_to_all x1, starting transfers between devices, share(): return lax.all_to_all(copies, 'rep', 0, 0, tiled=True)  4.02 us
  transfers between devices with their start and end apart: 2, of which 2 were waited for; matrix products, arithmetic and copies ran while one was open for 0% of the time, Pallas kernels for 1%

profile of v4, /device:TPU:1, one launch (start us, length us, event | category | flops | bytes accessed | tf_op | source)
XLA Modules:
  0.0 86.1 jit_solution(1782511271024926853)
XLA Ops:
  0.6 2.2 %shard_map.111 = (f32[128,128]{1,0:T(8,128)}, s32[8,1024]{1,0:T(8,128)}) custom-call(s32[1,1024]{1,0:T(1,128)} %bitcast.43, s32[2,512]{1,0:T(2,128)} %bitcast.44, f32[10,512]{1,0:T(8,128)} %moment2_hbm.1, s32[1,128]{1,0:T(1,128)} %rehome_hbm.1), custom_call_target="tpu_custom_call" | custom-call | tf_op jit(solution)/shard_map/pallas_call | solution.py:63
  2.9 0.0 copy-start
  2.9 0.0 copy-start.1
  2.9 0.0 copy-start.2
  2.9 0.0 copy-start.3
  2.9 18.6 %all-to-all-start.3 = ((f32[128,1,128]{2,1,0:T(1,128)}), f32[128,1,128]{2,1,0:T(1,128)S(1)}, u32[]{:S(2)}, u32[]{:S(2)}) async-start(f32[128,1,128]{2,1,0:T(1,128)} %bitcast.42), calls=%async_computation.3 | async-start | bytes 131072 | tf_op jit(solution)/shard_map/all_to_all | solution.py:549
  21.5 0.0 copy-start.4
  21.5 0.0 copy-done
  21.5 0.0 copy-done.1
  21.5 0.0 copy-done.2
  21.5 0.0 copy-done.3
  21.5 0.6 copy-done.4
  22.2 1.2 %shard_map.112 = (f32[16,512]{1,0:T(8,128)S(1)}, f32[96,128]{1,0:T(8,128)S(1)}, s32[8,1024]{1,0:T(8,128)S(1)}, f32[3,2,256]{2,1,0:T(2,128)S(1)}, bf16[512,512]{1,0:T(8,128)(2,1)S(1)}) custom-call(f32[10,512]{1,0:T(8,128)S(1)} %copy-done, f32[10,512]{1,0:T(8,128)S(1)} %copy-done.1, f32[1,8]{1,0:T(1,128)S(1)} %copy-done.4, s32[8,1024]{1,0:T(8,128)S(1)} %copy-done.2, ...), custom_call_target="tpu_custom_call" | custom-call | tf_op jit(solution)/shard_map/pallas_call | solution.py:63
  23.3 9.6 %all-to-all-done.3 = f32[128,1,128]{2,1,0:T(1,128)S(1)} async-done(((f32[128,1,128]{2,1,0:T(1,128)}), f32[128,1,128]{2,1,0:T(1,128)S(1)}, u32[]{:S(2)}, u32[]{:S(2)}) %all-to-all-start.3) | async-done | bytes 65568 | tf_op jit(solution)/shard_map/all_to_all | solution.py:549
  32.9 0.6 shard_map.113
  33.5 0.1 reshape.48
  33.6 17.9 %all_to_all.35 = f32[128,2,128]{2,1,0:T(2,128)S(1)} all-to-all(f32[128,2,128]{2,1,0:T(2,128)S(1)} %reshape.48), channel_id=1, replica_groups=mesh['dev'=128,'rep'=4] {'dev'}, dimensions={0} | all-to-all | bytes 262144 | tf_op jit(solution)/shard_map/all_to_all | solution.py:549
  51.5 4.2 %shard_map.114 = (f32[3,2,256]{2,1,0:T(2,128)}, f32[128,256]{1,0:T(8,128)S(1)}, f32[16,1024]{1,0:T(8,128)S(1)}) custom-call(f32[128,256]{1,0:T(8,128)S(1)} %bitcast.29, s32[8,1024]{1,0:T(8,128)S(1)} %get-tuple-element.54.lists_ref, f32[3,2,256]{2,1,0:T(2,128)S(1)} %get-tuple-element.55.target_ref), custom_call_target="tpu_custom_call" | custom-call | tf_op jit(solution)/shard_map/pallas_call | solution.py:63
  55.7 0.1 reshape.50
  55.8 17.8 %all_to_all.36 = f32[128,2,128]{2,1,0:T(2,128)S(1)} all-to-all(f32[128,2,128]{2,1,0:T(2,128)S(1)} %reshape.50), channel_id=1, replica_groups=mesh['dev'=128,'rep'=4] {'dev'}, dimensions={0} | all-to-all | bytes 262144 | tf_op jit(solution)/shard_map/all_to_all | solution.py:549
  73.5 1.8 %shard_map.115 = (f32[4,16,512]{2,1,0:T(8,128)}, f32[40,512]{1,0:T(8,128)S(1)}) custom-call(f32[128,256]{1,0:T(8,128)S(1)} %bitcast.31, f32[128,128]{1,0:T(8,128)S(1)} %bitcast.37, f32[128,256]{1,0:T(8,128)S(1)} %bitcast.30, f32[1,8]{1,0:T(1,128)S(1)} %copy-done.4), custom_call_target="tpu_custom_call" | custom-call | tf_op jit(solution)/shard_map/pallas_call | solution.py:63
  75.3 4.0 %all-to-all-start.6 = ((f32[4,16,512]{2,1,0:T(8,128)}), f32[4,16,512]{2,1,0:T(8,128)S(1)}, u32[]{:S(2)}, u32[]{:S(2)}) async-start(f32[4,16,512]{2,1,0:T(8,128)} %get-tuple-element.57), calls=%async_computation.6 | async-start | bytes 262144 | tf_op jit(solution)/shard_map/all_to_all | solution.py:553
  79.4 4.8 %all-to-all-done.6.grads_ref = f32[4,16,512]{2,1,0:T(8,128)S(1)} async-done(((f32[4,16,512]{2,1,0:T(8,128)}), f32[4,16,512]{2,1,0:T(8,128)S(1)}, u32[]{:S(2)}, u32[]{:S(2)}) %all-to-all-start.6) | async-done | bytes 131104 | tf_op jit(solution)/shard_map/all_to_all | solution.py:553
  84.2 0.9 %shard_map.116 = (f32[10,512]{1,0:T(8,128)}, f32[10,512]{1,0:T(8,128)}, f32[10,512]{1,0:T(8,128)}, s32[1,1]{1,0:T(1,128)}) custom-call(f32[4,16,512]{2,1,0:T(8,128)S(1)} %all-to-all-done.6.grads_ref, f32[40,512]{1,0:T(8,128)S(1)} %get-tuple-element.58.old_ref, bf16[512,512]{1,0:T(8,128)(2,1)S(1)} %get-tuple-element.59.order_ref), custom_call_target="tpu_custom_call" | custom-call | tf_op jit(solution)/shard_map/pallas_call | solution.py:63
  85.6 0.2 conditional.1
  (2 shorter events, 0.0 us)
Async XLA Ops:
  2.9 18.6 %copy-start = (f32[10,512]{1,0:T(8,128)S(1)}, f32[10,512]{1,0:T(8,128)}, u32[]{:S(2)}) copy-start(f32[10,512]{1,0:T(8,128)} %params_ref.1) | copy-start | bytes 61444
  2.9 18.6 %copy-start.1 = (f32[10,512]{1,0:T(8,128)S(1)}, f32[10,512]{1,0:T(8,128)}, u32[]{:S(2)}) copy-start(f32[10,512]{1,0:T(8,128)} %moment1_ref.1) | copy-start | bytes 61444
  2.9 18.6 %copy-start.2 = (s32[8,1024]{1,0:T(8,128)S(1)}, s32[8,1024]{1,0:T(8,128)}, u32[]{:S(2)}) copy-start(s32[8,1024]{1,0:T(8,128)} %get-tuple-element.51.lists_ref) | copy-start | bytes 98308
  2.9 18.6 %copy-start.3 = (f32[1,2,3,256]{3,1,2,0:T(2,128)S(1)}, f32[1,2,3,256]{3,1,2,0:T(2,128)}, u32[]{:S(2)}) copy-start(f32[1,2,3,256]{3,1,2,0:T(2,128)} %param.16) | copy-start | bytes 18436
  2.9 30.0 %all-to-all-start.3 = ((f32[128,1,128]{2,1,0:T(1,128)}), f32[128,1,128]{2,1,0:T(1,128)S(1)}, u32[]{:S(2)}, u32[]{:S(2)}) async-start(f32[128,1,128]{2,1,0:T(1,128)} %bitcast.42), calls=%async_computation.3 | async-start | bytes 131072 | tf_op jit(solution)/shard_map/all_to_all | solution.py:549
  21.5 0.7 copy-start.4
  75.3 8.8 %all-to-all-start.6 = ((f32[4,16,512]{2,1,0:T(8,128)}), f32[4,16,512]{2,1,0:T(8,128)S(1)}, u32[]{:S(2)}, u32[]{:S(2)}) async-start(f32[4,16,512]{2,1,0:T(8,128)} %get-tuple-element.57), calls=%async_computation.6 | async-start | bytes 262144 | tf_op jit(solution)/shard_map/all_to_all | solution.py:553

commit v5 on v4

--- a/solution.py
+++ b/solution.py
@@ -629,9 +629,12 @@
         )(exchange(sent), old, camera)
         return list(update(share(sent), old, order)[:3])
 
-    out = lax.cond(
-        full[0, 0] > 0, by_owner, lambda out, *rest: out,
-        list(out), by_entry, lists, request, old, order, camera,
+    _, out = lax.while_loop(
+        lambda carry: carry[0] > 0,
+        lambda carry: (
+            jnp.int32(0), by_owner(carry[1], by_entry, lists, request, old, order, camera)
+        ),
+        (full[0, 0], list(out)),
     )
     return (*out, images.transpose(1, 0, 2)[None])
 

time: 86.5 us -> 85.8 us (level)
  blocking collectives: 35.7 us -> 44.3 us
  waiting for transfers between devices: 14.4 us -> 9.59 us
  starting transfers between devices: 22.6 us -> 18.6 us
    all_to_all x0 -> x1, blocking collectives: none -> 8.64 us  [share(): return lax.all_to_all(copies, 'rep', 0, 0, tiled=True)]
    all_to_all x1 -> x0, waiting for transfers between devices: 4.83 us -> none  [share(): return lax.all_to_all(copies, 'rep', 0, 0, tiled=True)]
    all_to_all x1 -> x0, starting transfers between devices: 4.02 us -> none  [share(): return lax.all_to_all(copies, 'rep', 0, 0, tiled=True)]
  transfers between devices with their start and end apart: 2 -> 1, of which waited for: 2 -> 1; matrix products, arithmetic and copies ran while one was open for 0% -> 0% of each run, Pallas kernels for 1% -> 1%
where the time goes in v5:
time: 85.8 us; the launch traced here: 85.4 us
  blocking collectives  44.3 us (52%)
  starting transfers between devices  18.6 us (22%)
  Pallas kernels  10.4 us (12%)
  waiting for transfers between devices  9.59 us (11%)
  between operations  0.93 us (1%)
    all_to_all x2, blocking collectives, exchange(): return lax.all_to_all(parcel, 'dev', 0, 0, tiled=True).reshape(x.shape)  35.7 us
    all_to_all x1, starting transfers between devices, exchange(): return lax.all_to_all(parcel, 'dev', 0, 0, tiled=True).reshape(x.shape)  18.6 us
    pallas_call x6, Pallas kernels, run(): pl.pallas_call(body, out_shape=out_shape, in_specs=[pl.BlockSpec(memory_s...  10.4 us
    all_to_all x1, waiting for transfers between devices, exchange(): return lax.all_to_all(parcel, 'dev', 0, 0, tiled=True).reshape(x.shape)  9.59 us
    all_to_all x1, blocking collectives, share(): return lax.all_to_all(copies, 'rep', 0, 0, tiled=True)  8.64 us
  transfers between devices with their start and end apart: 1, of which 1 were waited for; matrix products, arithmetic and copies ran while one was open for 0% of the time, Pallas kernels for 1%

profile of v5, /device:TPU:1, one launch (start us, length us, event | category | flops | bytes accessed | tf_op | source)
XLA Modules:
  0.0 85.4 jit_solution(13131058065752974675)
XLA Ops:
  0.6 2.2 %shard_map.111 = (f32[128,128]{1,0:T(8,128)}, s32[8,1024]{1,0:T(8,128)}) custom-call(s32[1,1024]{1,0:T(1,128)} %bitcast.43, s32[2,512]{1,0:T(2,128)} %bitcast.44, f32[10,512]{1,0:T(8,128)} %moment2_hbm.1, s32[1,128]{1,0:T(1,128)} %rehome_hbm.1), custom_call_target="tpu_custom_call" | custom-call | tf_op jit(solution)/shard_map/pallas_call | solution.py:63
  2.9 0.0 copy-start
  2.9 0.0 copy-start.1
  2.9 0.0 copy-start.2
  2.9 0.0 copy-start.3
  2.9 18.6 %all-to-all-start.3 = ((f32[128,1,128]{2,1,0:T(1,128)}), f32[128,1,128]{2,1,0:T(1,128)S(1)}, u32[]{:S(2)}, u32[]{:S(2)}) async-start(f32[128,1,128]{2,1,0:T(1,128)} %bitcast.42), calls=%async_computation.3 | async-start | bytes 131072 | tf_op jit(solution)/shard_map/all_to_all | solution.py:549
  21.5 0.0 copy-start.4
  21.5 0.0 copy-done
  21.5 0.0 copy-done.1
  21.5 0.0 copy-done.2
  21.5 0.0 copy-done.3
  21.5 0.6 copy-done.4
  22.1 1.2 %shard_map.112 = (f32[16,512]{1,0:T(8,128)S(1)}, f32[96,128]{1,0:T(8,128)S(1)}, s32[8,1024]{1,0:T(8,128)S(1)}, f32[3,2,256]{2,1,0:T(2,128)S(1)}, bf16[512,512]{1,0:T(8,128)(2,1)S(1)}) custom-call(f32[10,512]{1,0:T(8,128)S(1)} %copy-done, f32[10,512]{1,0:T(8,128)S(1)} %copy-done.1, f32[1,8]{1,0:T(1,128)S(1)} %copy-done.4, s32[8,1024]{1,0:T(8,128)S(1)} %copy-done.2, ...), custom_call_target="tpu_custom_call" | custom-call | tf_op jit(solution)/shard_map/pallas_call | solution.py:63
  23.3 9.6 %all-to-all-done.3 = f32[128,1,128]{2,1,0:T(1,128)S(1)} async-done(((f32[128,1,128]{2,1,0:T(1,128)}), f32[128,1,128]{2,1,0:T(1,128)S(1)}, u32[]{:S(2)}, u32[]{:S(2)}) %all-to-all-start.3) | async-done | bytes 65568 | tf_op jit(solution)/shard_map/all_to_all | solution.py:549
  32.9 0.5 shard_map.113
  33.5 0.1 reshape.44
  33.6 17.9 %all_to_all.34 = f32[128,2,128]{2,1,0:T(2,128)S(1)} all-to-all(f32[128,2,128]{2,1,0:T(2,128)S(1)} %reshape.44), channel_id=1, replica_groups=mesh['dev'=128,'rep'=4] {'dev'}, dimensions={0} | all-to-all | bytes 262144 | tf_op jit(solution)/shard_map/all_to_all | solution.py:549
  51.5 4.2 %shard_map.114 = (f32[3,2,256]{2,1,0:T(2,128)}, f32[128,256]{1,0:T(8,128)S(1)}, f32[16,1024]{1,0:T(8,128)S(1)}) custom-call(f32[128,256]{1,0:T(8,128)S(1)} %bitcast.32, s32[8,1024]{1,0:T(8,128)S(1)} %get-tuple-element.127.lists_ref, f32[3,2,256]{2,1,0:T(2,128)S(1)} %get-tuple-element.78.target_ref), custom_call_target="tpu_custom_call" | custom-call | tf_op jit(solution)/shard_map/pallas_call | solution.py:63
  55.7 0.1 reshape.46
  55.8 17.7 %all_to_all.35 = f32[128,2,128]{2,1,0:T(2,128)S(1)} all-to-all(f32[128,2,128]{2,1,0:T(2,128)S(1)} %reshape.46), channel_id=1, replica_groups=mesh['dev'=128,'rep'=4] {'dev'}, dimensions={0} | all-to-all | bytes 262144 | tf_op jit(solution)/shard_map/all_to_all | solution.py:549
  73.5 1.3 %shard_map.115 = (f32[4,16,512]{2,1,0:T(8,128)S(1)}, f32[40,512]{1,0:T(8,128)S(1)}) custom-call(f32[128,256]{1,0:T(8,128)S(1)} %bitcast.34, f32[128,128]{1,0:T(8,128)S(1)} %bitcast.38, f32[128,256]{1,0:T(8,128)S(1)} %bitcast.33, f32[1,8]{1,0:T(1,128)S(1)} %copy-done.4), custom_call_target="tpu_custom_call" | custom-call | tf_op jit(solution)/shard_map/pallas_call | solution.py:63
  74.9 8.6 %all_to_all.36.grads_ref = f32[4,16,512]{2,1,0:T(8,128)S(1)} all-to-all(f32[4,16,512]{2,1,0:T(8,128)S(1)} %get-tuple-element.80), channel_id=1, replica_groups=mesh['dev'=128,'rep'=4] {'rep'}, dimensions={0} | all-to-all | bytes 262144 | tf_op jit(solution)/shard_map/all_to_all | solution.py:553
  83.5 0.9 %shard_map.116 = (f32[10,512]{1,0:T(8,128)}, f32[10,512]{1,0:T(8,128)}, f32[10,512]{1,0:T(8,128)}, s32[1,1]{1,0:T(1,128)}) custom-call(f32[4,16,512]{2,1,0:T(8,128)S(1)} %all_to_all.36.grads_ref, f32[40,512]{1,0:T(8,128)S(1)} %get-tuple-element.129.old_ref, bf16[512,512]{1,0:T(8,128)(2,1)S(1)} %get-tuple-element.131.order_ref), custom_call_target="tpu_custom_call" | custom-call | tf_op jit(solution)/shard_map/pallas_call | solution.py:63
  84.4 0.8 while.13
  (2 shorter events, 0.0 us)
Async XLA Ops:
  2.9 18.6 %copy-start = (f32[10,512]{1,0:T(8,128)S(1)}, f32[10,512]{1,0:T(8,128)}, u32[]{:S(2)}) copy-start(f32[10,512]{1,0:T(8,128)} %params_ref.1) | copy-start | bytes 61444
  2.9 18.6 %copy-start.1 = (f32[10,512]{1,0:T(8,128)S(1)}, f32[10,512]{1,0:T(8,128)}, u32[]{:S(2)}) copy-start(f32[10,512]{1,0:T(8,128)} %moment1_ref.1) | copy-start | bytes 61444
  2.9 18.6 %copy-start.2 = (s32[8,1024]{1,0:T(8,128)S(1)}, s32[8,1024]{1,0:T(8,128)}, u32[]{:S(2)}) copy-start(s32[8,1024]{1,0:T(8,128)} %get-tuple-element.74.lists_ref) | copy-start | bytes 98308
  2.9 18.6 %copy-start.3 = (f32[1,2,3,256]{3,1,2,0:T(2,128)S(1)}, f32[1,2,3,256]{3,1,2,0:T(2,128)}, u32[]{:S(2)}) copy-start(f32[1,2,3,256]{3,1,2,0:T(2,128)} %param.16) | copy-start | bytes 18436
  2.9 30.0 %all-to-all-start.3 = ((f32[128,1,128]{2,1,0:T(1,128)}), f32[128,1,128]{2,1,0:T(1,128)S(1)}, u32[]{:S(2)}, u32[]{:S(2)}) async-start(f32[128,1,128]{2,1,0:T(1,128)} %bitcast.42), calls=%async_computation.3 | async-start | bytes 131072 | tf_op jit(solution)/shard_map/all_to_all | solution.py:549
  21.5 0.7 copy-start.4

commit v6 on v5

--- a/solution.py
+++ b/solution.py
@@ -452,8 +452,15 @@
     out_ref[6:10] = total[5:9] * level * (1.0 - level)
 
 
+def spread_copies(total_s, out_ref):
+    total = total_s[0:12]
+    for copy in range(out_ref.shape[0]):
+        for i in range(total.shape[1] // 128):
+            out_ref[copy, i * 12 : i * 12 + 12] = total[:, i * 128 : i * 128 + 128]
+
+
 def collect_body(
-    grad_ref, request_ref, response_ref, camera_ref, out_hbm, old_ref, came_s, total_s, sems
+    grad_ref, request_ref, response_ref, camera_ref, out_ref, old_ref, came_s, total_s
 ):
     settle(request_ref, response_ref, old_ref)
     devices = grad_ref.shape[0]
@@ -480,9 +487,7 @@
     flags = came_s[SENT * HOME_CAP :]
     flag = jnp.max(jnp.max(flags, axis=1, keepdims=True), axis=0, keepdims=True)
     total_s[10:11] = flag + jnp.zeros((1, total_s.shape[1]), F32)
-    copies = [start(total_s, out_hbm.at[n], sems.at[n]) for n in range(out_hbm.shape[0])]
-    for copy in copies:
-        copy.wait()
+    spread_copies(total_s, out_ref)
 
 
 def to_owner_body(entry_ref, lists_ref, out_ref):
@@ -515,8 +520,7 @@
     total = jnp.concatenate([came[i * 32 : i * 32 + ROWS] for i in range(sub)], axis=1)
     total_s[...] = jnp.zeros_like(total_s)
     pull_back(total, old_ref[...], camera_ref, total_s)
-    for copy in range(out_ref.shape[0]):
-        out_ref[copy] = total_s[...]
+    spread_copies(total_s, out_ref)
 
 
 def adam_body(
@@ -524,6 +528,7 @@
 ):
     old = old_ref[...]
     grad = (grads_ref[0] + grads_ref[1]) + (grads_ref[2] + grads_ref[3])
+    grad = jnp.concatenate([grad[n : n + 12] for n in range(0, grad.shape[0], 12)], axis=1)
     full_ref[0, 0] = (jnp.max(grad[10:11]) > 0.5).astype(jnp.int32)
     grad = grad[0:10]
     moment1 = 0.9 * old[10:20] + 0.1 * grad
@@ -603,13 +608,11 @@
     grads = exchange(grads)
     grads, old = call(
         collect_body,
-        (shape(reps, ROWS, gauss), shape(40, gauss)),
+        (shape(reps, gauss * 12 // 128, 128), shape(40, gauss)),
         [
             pltpu.VMEM((256, devices), F32), pltpu.VMEM((ROWS, gauss), F32),
-            pltpu.SemaphoreType.DMA((reps,)),
         ],
         smem=(3,),
-        hbm_out=(0,),
     )(grads, request, response, camera)
     update = call(
         adam_body,
@@ -625,7 +628,7 @@
             exchange(sent), request, lists
         )
         sent = call(
-            at_home_body, shape(reps, ROWS, gauss), [pltpu.VMEM((ROWS, gauss), F32)], smem=(2,)
+            at_home_body, shape(reps, gauss * 12 // 128, 128), [pltpu.VMEM((ROWS, gauss), F32)], smem=(2,)
         )(exchange(sent), old, camera)
         return list(update(share(sent), old, order)[:3])
 

time: 85.8 us -> 85.4 us (level)
  no operation moved by 1% of the time
where the time goes in v6:
time: 85.4 us; the launch traced here: 85 us
  blocking collectives  44.2 us (52%)
  starting transfers between devices  18.6 us (22%)
  Pallas kernels  10.2 us (12%)
  waiting for transfers between devices  9.59 us (11%)
  between operations  0.92 us (1%)
    all_to_all x2, blocking collectives, exchange(): return lax.all_to_all(parcel, 'dev', 0, 0, tiled=True).reshape(x.shape)  35.7 us
    all_to_all x1, starting transfers between devices, exchange(): return lax.all_to_all(parcel, 'dev', 0, 0, tiled=True).reshape(x.shape)  18.6 us
    pallas_call x6, Pallas kernels, run(): pl.pallas_call(body, out_shape=out_shape, in_specs=[pl.BlockSpec(memory_s...  10.2 us
    all_to_all x1, waiting for transfers between devices, exchange(): return lax.all_to_all(parcel, 'dev', 0, 0, tiled=True).reshape(x.shape)  9.59 us
    all_to_all x1, blocking collectives, share(): return lax.all_to_all(copies, 'rep', 0, 0, tiled=True)  8.46 us
  transfers between devices with their start and end apart: 1, of which 1 were waited for; matrix products, arithmetic and copies ran while one was open for 0% of the time, Pallas kernels for 1%

profile of v6, /device:TPU:1, one launch (start us, length us, event | category | flops | bytes accessed | tf_op | source)
XLA Modules:
  0.0 85.0 jit_solution(1843561028881031241)
XLA Ops:
  0.6 2.2 %shard_map.111 = (f32[128,128]{1,0:T(8,128)}, s32[8,1024]{1,0:T(8,128)}) custom-call(s32[1,1024]{1,0:T(1,128)} %bitcast.43, s32[2,512]{1,0:T(2,128)} %bitcast.44, f32[10,512]{1,0:T(8,128)} %moment2_hbm.1, s32[1,128]{1,0:T(1,128)} %rehome_hbm.1), custom_call_target="tpu_custom_call" | custom-call | tf_op jit(solution)/shard_map/pallas_call | solution.py:63
  2.9 0.0 copy-start
  2.9 0.0 copy-start.1
  2.9 0.0 copy-start.2
  2.9 0.0 copy-start.3
  2.9 18.6 %all-to-all-start.3 = ((f32[128,1,128]{2,1,0:T(1,128)}), f32[128,1,128]{2,1,0:T(1,128)S(1)}, u32[]{:S(2)}, u32[]{:S(2)}) async-start(f32[128,1,128]{2,1,0:T(1,128)} %bitcast.42), calls=%async_computation.3 | async-start | bytes 131072 | tf_op jit(solution)/shard_map/all_to_all | solution.py:554
  21.5 0.0 copy-start.4
  21.5 0.0 copy-done
  21.5 0.0 copy-done.1
  21.5 0.0 copy-done.2
  21.5 0.0 copy-done.3
  21.5 0.6 copy-done.4
  22.1 1.2 %shard_map.112 = (f32[16,512]{1,0:T(8,128)S(1)}, f32[96,128]{1,0:T(8,128)S(1)}, s32[8,1024]{1,0:T(8,128)S(1)}, f32[3,2,256]{2,1,0:T(2,128)S(1)}, bf16[512,512]{1,0:T(8,128)(2,1)S(1)}) custom-call(f32[10,512]{1,0:T(8,128)S(1)} %copy-done, f32[10,512]{1,0:T(8,128)S(1)} %copy-done.1, f32[1,8]{1,0:T(1,128)S(1)} %copy-done.4, s32[8,1024]{1,0:T(8,128)S(1)} %copy-done.2, ...), custom_call_target="tpu_custom_call" | custom-call | tf_op jit(solution)/shard_map/pallas_call | solution.py:63
  23.3 9.6 %all-to-all-done.3 = f32[128,1,128]{2,1,0:T(1,128)S(1)} async-done(((f32[128,1,128]{2,1,0:T(1,128)}), f32[128,1,128]{2,1,0:T(1,128)S(1)}, u32[]{:S(2)}, u32[]{:S(2)}) %all-to-all-start.3) | async-done | bytes 65568 | tf_op jit(solution)/shard_map/all_to_all | solution.py:554
  32.9 0.5 shard_map.113
  33.5 0.1 reshape.44
  33.6 17.9 %all_to_all.34 = f32[128,2,128]{2,1,0:T(2,128)S(1)} all-to-all(f32[128,2,128]{2,1,0:T(2,128)S(1)} %reshape.44), channel_id=1, replica_groups=mesh['dev'=128,'rep'=4] {'dev'}, dimensions={0} | all-to-all | bytes 262144 | tf_op jit(solution)/shard_map/all_to_all | solution.py:554
  51.5 4.2 %shard_map.114 = (f32[3,2,256]{2,1,0:T(2,128)}, f32[128,256]{1,0:T(8,128)S(1)}, f32[16,1024]{1,0:T(8,128)S(1)}) custom-call(f32[128,256]{1,0:T(8,128)S(1)} %bitcast.32, s32[8,1024]{1,0:T(8,128)S(1)} %get-tuple-element.127.lists_ref, f32[3,2,256]{2,1,0:T(2,128)S(1)} %get-tuple-element.78.target_ref), custom_call_target="tpu_custom_call" | custom-call | tf_op jit(solution)/shard_map/pallas_call | solution.py:63
  55.7 0.1 reshape.46
  55.8 17.7 %all_to_all.35 = f32[128,2,128]{2,1,0:T(2,128)S(1)} all-to-all(f32[128,2,128]{2,1,0:T(2,128)S(1)} %reshape.46), channel_id=1, replica_groups=mesh['dev'=128,'rep'=4] {'dev'}, dimensions={0} | all-to-all | bytes 262144 | tf_op jit(solution)/shard_map/all_to_all | solution.py:554
  73.5 1.1 %shard_map.115 = (f32[4,48,128]{2,1,0:T(8,128)S(1)}, f32[40,512]{1,0:T(8,128)S(1)}) custom-call(f32[128,256]{1,0:T(8,128)S(1)} %bitcast.34, f32[128,128]{1,0:T(8,128)S(1)} %bitcast.38, f32[128,256]{1,0:T(8,128)S(1)} %bitcast.33, f32[1,8]{1,0:T(1,128)S(1)} %copy-done.4), custom_call_target="tpu_custom_call" | custom-call | tf_op jit(solution)/shard_map/pallas_call | solution.py:63
  74.7 8.5 %all_to_all.36.grads_ref = f32[4,48,128]{2,1,0:T(8,128)S(1)} all-to-all(f32[4,48,128]{2,1,0:T(8,128)S(1)} %get-tuple-element.80), channel_id=1, replica_groups=mesh['dev'=128,'rep'=4] {'rep'}, dimensions={0} | all-to-all | bytes 196608 | tf_op jit(solution)/shard_map/all_to_all | solution.py:558
  83.1 0.9 %shard_map.116 = (f32[10,512]{1,0:T(8,128)}, f32[10,512]{1,0:T(8,128)}, f32[10,512]{1,0:T(8,128)}, s32[1,1]{1,0:T(1,128)}) custom-call(f32[4,48,128]{2,1,0:T(8,128)S(1)} %all_to_all.36.grads_ref, f32[40,512]{1,0:T(8,128)S(1)} %get-tuple-element.129.old_ref, bf16[512,512]{1,0:T(8,128)(2,1)S(1)} %get-tuple-element.131.order_ref), custom_call_target="tpu_custom_call" | custom-call | tf_op jit(solution)/shard_map/pallas_call | solution.py:63
  84.0 0.8 while.13
  (2 shorter events, 0.0 us)
Async XLA Ops:
  2.9 18.6 %copy-start = (f32[10,512]{1,0:T(8,128)S(1)}, f32[10,512]{1,0:T(8,128)}, u32[]{:S(2)}) copy-start(f32[10,512]{1,0:T(8,128)} %params_ref.1) | copy-start | bytes 61444
  2.9 18.6 %copy-start.1 = (f32[10,512]{1,0:T(8,128)S(1)}, f32[10,512]{1,0:T(8,128)}, u32[]{:S(2)}) copy-start(f32[10,512]{1,0:T(8,128)} %moment1_ref.1) | copy-start | bytes 61444
  2.9 18.6 %copy-start.2 = (s32[8,1024]{1,0:T(8,128)S(1)}, s32[8,1024]{1,0:T(8,128)}, u32[]{:S(2)}) copy-start(s32[8,1024]{1,0:T(8,128)} %get-tuple-element.74.lists_ref) | copy-start | bytes 98308
  2.9 18.6 %copy-start.3 = (f32[1,2,3,256]{3,1,2,0:T(2,128)S(1)}, f32[1,2,3,256]{3,1,2,0:T(2,128)}, u32[]{:S(2)}) copy-start(f32[1,2,3,256]{3,1,2,0:T(2,128)} %param.16) | copy-start | bytes 18436
  2.9 30.0 %all-to-all-start.3 = ((f32[128,1,128]{2,1,0:T(1,128)}), f32[128,1,128]{2,1,0:T(1,128)S(1)}, u32[]{:S(2)}, u32[]{:S(2)}) async-start(f32[128,1,128]{2,1,0:T(1,128)} %bitcast.42), calls=%async_computation.3 | async-start | bytes 131072 | tf_op jit(solution)/shard_map/all_to_all | solution.py:554
  21.5 0.7 copy-start.4
